TPU v7x, 256 devices: a whole 4x4x8 slice. The times are simulated.
256 devices in a mesh: row: 8 (over z_lo, core), col: 32 (over x, y, z_hi).
Axes of the slice: x: 4, y: 4, z: 8 (z_hi: 2, z_lo: 4; z = z_hi * 4 + z_lo), core: 2. Of those that a mesh axis runs over, the one named last changes fastest.
Arguments:
- mat_a: bfloat16 [20480, 49152], P('row', 'col'), may hold values from -6 to 6
- mat_b: bfloat16 [49152, 8192], P('row', 'col'), may hold values from -0.15625 to 0.15625
- mask_a: int32 [160, 384], P('row', 'col'), may hold values from 0 to 1, as said below
- mask_b: int32 [384, 64], P('row', 'col'), may hold values 0 or 1
Outputs:
- product: bfloat16 [20480, 8192], P('row', 'col')
Inputs may be any that keep to these rules, and one draw needn't show every extreme that they name: `mask_a`: in each tile of 20 x 12 entries, the block rows holding an occupied block come first and each holds at least one; in every draw some tile has all 20 block rows occupied.
All inputs are finite; a program needn't handle non-finite values. No bound on the sum of `mask_b` on one device may be relied on, other than what follows from the above.
Results may differ from a plain program's by a relative error of at most 0.0025.
Values may be sent and summed in bfloat16 or wider, within the bound.
No kernel may reach another device: no remote copies, remote signals or barrier semaphores. Data moves between devices by JAX's collectives and lax.ppermute only.
A program may use at most 128 MiB of HBM per device.

v0:
```python
import jax
import jax.numpy as jnp
from jax import lax
from jax.sharding import PartitionSpec as P

BLK = 128


def from_behind(value, axis, steps):
    count = lax.axis_size(axis)
    pairs = [(source, (source + steps) % count) for source in range(count)]
    return lax.ppermute(value, axis, pairs)


def mask_blocks(matrix, occupied):
    rows, columns = occupied.shape
    blocked = matrix.reshape(rows, matrix.shape[0] // rows, columns, matrix.shape[1] // columns)
    scaling = occupied.astype(matrix.dtype)[:, None, :, None]
    return (blocked * scaling).reshape(matrix.shape)


def live_rows(occupied):
    return jnp.sum(jnp.any(occupied > 0, axis=1).astype(jnp.int32))


def add_rows(accum, matrix_rows, right_tile, row_first, row_last):
    block = BLK

    def one_row(row_index, summed):
        row_block = lax.dynamic_slice_in_dim(matrix_rows, row_index * block, block, 0)
        result = jnp.dot(row_block, right_tile, preferred_element_type=jnp.float32)
        current = lax.dynamic_slice_in_dim(summed, row_index * block, block, 0)
        return lax.dynamic_update_slice_in_dim(summed, current + result, row_index * block, 0)

    return lax.fori_loop(row_first, row_last, one_row, accum)


def body(mat_a, mat_b, mask_a, mask_b):
    inner_rows = mat_a.shape[1]
    inner_blocks = mask_a.shape[1]
    flags_a = mask_a.astype(jnp.bfloat16)
    flags_b = mask_b.astype(jnp.bfloat16)
    own_a = mask_blocks(mat_a, mask_a)
    own_b = mask_blocks(mat_b[:inner_rows], mask_b[:inner_blocks])
    row_place = lax.axis_index("row")
    slot_pick = jnp.where(row_place == 0, 1, 0).astype(jnp.int32)
    send_b = lax.dynamic_slice_in_dim(mat_b, slot_pick * inner_rows, inner_rows, 0)
    send_flags = lax.dynamic_slice_in_dim(flags_b, slot_pick * inner_blocks, inner_blocks, 0)
    live_here = live_rows(mask_a)
    accum = jnp.zeros((mat_a.shape[0], mat_b.shape[1]), jnp.float32)
    next_a, next_flags = from_behind((mat_a, flags_a), "col", -1)
    live_next = live_rows(next_flags)
    next_b, next_marks = from_behind((send_b, send_flags), "row", -1)
    accum = add_rows(accum, own_a, own_b, 0, live_here)
    accum = add_rows(
        accum, mask_blocks(next_a, next_flags), mask_blocks(next_b, next_marks), 0, live_next
    )
    return accum.astype(jnp.bfloat16)


def solution(mesh):
    return jax.shard_map(
        body,
        mesh=mesh,
        in_specs=(P("row", "col"), P("row", "col"), P("row", "col"), P("row", "col")),
        out_specs=P("row", "col"),
        check_vma=False,
    )
```

profile of v0, /device:TPU:0, one launch (start us, length us, event | category | flops | bytes accessed | tf_op | source)
XLA Modules:
  0.0 420.9 jit_solution(16425240964362362557)
XLA Ops:
  0.0 10.6 %copy.9 = bf16[2560,1536]{0,1:T(8,128)(2,1)} copy(bf16[2560,1536]{1,0:T(8,128)(2,1)} %param.8) | data formatting | bytes 15728640 | tf_op args[0]
  10.6 10.1 %collective-permute-start.1 = (bf16[2560,1536]{0,1:T(8,128)(2,1)}, bf16[2560,1536]{0,1:T(8,128)(2,1)}, u32[]{:S(2)}, u32[]{:S(2)}) collective-permute-start(bf16[2560,1536]{0,1:T(8,128)(2,1)} %copy.9), channel_id=1, source_target_pairs={{0,31},{1,0},{2,1},{3,2},{4,3},{5,4},{6,5},{7,6},{8,7},{9,8},{10,9... | collective-permute-start | bytes 23592968 | tf_op jit(solution)/shard_map/ppermute | solution.py:12
  21.5 2.5 constant_dynamic-slice_fusion.1
  24.0 2.2 collective-permute-start.2
  30.7 3.8 bitcast_multiply_fusion.1
  34.5 1.7 broadcast_in_dim.2
  36.2 3.3 while.20
  36.9 2.0 fusion.16
  39.5 329.7 %collective-permute-done.3 = bf16[12,2]{0,1:T(2,128)(2,1)S(1)} collective-permute-done((bf16[12,2]{0,1:T(2,128)(2,1)S(1)}, bf16[12,2]{0,1:T(2,128)(2,1)S(1)}, u32[]{:S(2)}, u32[]{:S(2)}) %collective-permute-start.3) | collective-permute-done | bytes 80 | tf_op jit(solution)/shard_map/ppermute | solution.py:12
  372.0 7.3 %bitcast_multiply_fusion = bf16[2560,1536]{0,1:T(8,128)(2,1)} fusion(bf16[2560,1536]{0,1:T(8,128)(2,1)} %collective-permute-done.1, bf16[192,8,20,128]{3,2,1,0:T(8,128)(2,1)S(1)} %bitcast.26), kind=kLoop, calls=%fused_computation.8 | loop fusion | flops 3932160 | bytes 23592960 | tf_op jit(solution)/shard_map/mul | solution.py:19
  379.3 40.4 %while.21 = (s32[]{:T(128)}, f32[2560,256]{1,0:T(8,128)S(1)}, s32[]{:T(128)}, bf16[2560,1536]{0,1:T(8,128)(2,1)}, bf16[1536,256]{1,0:T(8,128)(2,1)S(1)}, /*index=5*/s32[]{:T(128)}, s32[]{:T(128)}, s32[]{:T(128)}, s32[]{:T(128)}) while((s32[]{:T(128)}, f32[2560,256]{1,0:T(8,128)S(1)}, s32[]{:T(128)}, bf16[2560,1536]{0,1:T(8,128)(2,1)}, ...), condition=%wide.region_7.8_spmd, body=%wide.region_6.7_spmd.sunk | while | flops 100696072 | bytes 1442963 | solution.py:35
  380.0 1.3 fusion.19
  382.0 1.3 fusion.19
  384.0 1.3 fusion.19
  387.9 1.3 fusion.19
  389.9 1.3 fusion.19
  395.9 1.3 fusion.19
  397.9 1.3 fusion.19
  399.9 1.3 fusion.19
  405.8 1.3 fusion.19
  407.8 1.3 fusion.19
  409.8 1.3 fusion.19
  415.7 1.3 fusion.19
  417.7 1.3 fusion.19
  (35 shorter events, 18.4 us)
Async XLA Ops:
  0.0 20.7 %copy-start.2 = (s32[20,12]{0,1:T(8,128)S(1)}, s32[20,12]{0,1:T(8,128)}, u32[]{:S(2)}) copy-start(s32[20,12]{0,1:T(8,128)} %param.10) | copy-start | bytes 2884
  0.0 20.8 %copy-start.3 = (s32[48,2]{0,1:T(2,128)S(1)}, s32[48,2]{0,1:T(2,128)}, u32[]{:S(2)}) copy-start(s32[48,2]{0,1:T(2,128)} %param.11) | copy-start | bytes 1156
  10.6 360.1 %collective-permute-start.1 = (bf16[2560,1536]{0,1:T(8,128)(2,1)}, bf16[2560,1536]{0,1:T(8,128)(2,1)}, u32[]{:S(2)}, u32[]{:S(2)}) collective-permute-start(bf16[2560,1536]{0,1:T(8,128)(2,1)} %copy.9), channel_id=1, source_target_pairs={{0,31},{1,0},{2,1},{3,2},{4,3},{5,4},{6,5},{7,6},{8,7},{9,8},{10,9... | collective-permute-start | bytes 23592968 | tf_op jit(solution)/shard_map/ppermute | solution.py:12
  20.7 348.6 %collective-permute-start = (bf16[20,12]{0,1:T(8,128)(2,1)S(1)}, bf16[20,12]{0,1:T(8,128)(2,1)S(1)}, u32[]{:S(2)}, u32[]{:S(2)}) collective-permute-start(bf16[20,12]{0,1:T(8,128)(2,1)S(1)} %convert_element_type.16), channel_id=1, source_target_pairs={{0,31},{1,0},{2,1},{3,2},{4,3},{5,4},{6,5},{7,6},{8,7},{9,8},{10,9... | collective-permute-start | bytes 1448 | tf_op jit(solution)/shard_map/ppermute | solution.py:12
  24.0 346.0 %collective-permute-start.2 = (bf16[1536,256]{1,0:T(8,128)(2,1)}, bf16[1536,256]{1,0:T(8,128)(2,1)S(1)}, u32[]{:S(2)}, u32[]{:S(2)}) collective-permute-start(bf16[1536,256]{1,0:T(8,128)(2,1)} %get-tuple-element.93), channel_id=1, source_target_pairs={{0,224},{32,0},{64,32},{96,64},{128,96},{160,128},{192,160},{224,1... | collective-permute-start | bytes 2359304 | tf_op jit(solution)/shard_map/ppermute | solution.py:12
  26.2 343.0 %collective-permute-start.3 = (bf16[12,2]{0,1:T(2,128)(2,1)S(1)}, bf16[12,2]{0,1:T(2,128)(2,1)S(1)}, u32[]{:S(2)}, u32[]{:S(2)}) collective-permute-start(bf16[12,2]{0,1:T(2,128)(2,1)S(1)} %get-tuple-element.95), channel_id=1, source_target_pairs={{0,224},{32,0},{64,32},{96,64},{128,96},{160,128},{192,160},{224,1... | collective-permute-start | bytes 152 | tf_op jit(solution)/shard_map/ppermute | solution.py:12
  27.5 3.2 copy-start
  372.0 7.3 %copy-start.1 = (f32[2560,256]{1,0:T(8,128)S(1)}, f32[2560,256]{1,0:T(8,128)}, u32[]{:S(2)}) copy-start(f32[2560,256]{1,0:T(8,128)} %get-tuple-element.189) | copy-start | bytes 7864324
where the time goes:
time: 423 us; the launch traced here: 421 us
  waiting for transfers between devices  330 us (78%)
  matrix products  28.5 us (7%)
  local copies, waits for them, and re-layouts  17.4 us (4%)
  other arithmetic  16.5 us (4%)
  loops' own time  15.1 us (4%)
  starting transfers between devices  13.6 us (3%)
    ppermute x4, waiting for transfers between devices, from_behind(): return lax.ppermute(value, axis, pairs)  330 us
    dot_general x21, matrix products, one_row(): result = jnp.dot(row_block, right_tile, preferred_element_type=jnp.float32)  28.5 us
    another operation x2, loops' own time, add_rows(): return lax.fori_loop(row_first, row_last, one_row, accum)  15.1 us
    ppermute x4, starting transfers between devices, from_behind(): return lax.ppermute(value, axis, pairs)  13.6 us
    unnamed x9, local copies, waits for them, and re-layouts  11.9 us
    mul x3, other arithmetic, mask_blocks(): return (blocked * scaling).reshape(matrix.shape)  11.3 us
  transfers between devices with their start and end apart: 4, of which 1 were waited for; matrix products, arithmetic and copies ran while one was open for 3% of the time, Pallas kernels for 0%

commit v1 on v0

v1 whole, which is shorter than its diff:
```python
import functools

import jax
import jax.numpy as jnp
from jax import lax
from jax.experimental import pallas as pl
from jax.experimental.pallas import tpu as pltpu
from jax.sharding import PartitionSpec as P

BLK = 128
STEP_BLOCKS = 5
PAD = 16
HALVES = 2
VMEM = 60 * 1024 * 1024


def masked(block, flag):
    return jnp.where(flag > 0, block, jnp.zeros_like(block))


def pick_kernel(slot_ref, mask_ref, b_ref, out_ref, *, blocks):
    base = slot_ref[0] * blocks
    for k in range(blocks):
        for c in range(out_ref.shape[1] // BLK):
            rows, cols = pl.ds(k * BLK, BLK), pl.ds(c * BLK, BLK)
            out_ref[rows, cols] = masked(b_ref[rows, cols], mask_ref[base + k, c])


def pick_b(mat_b, mask_b, slot, depth):
    columns = mat_b.shape[1]
    return pl.pallas_call(
        functools.partial(pick_kernel, blocks=depth // BLK),
        grid_spec=pltpu.PrefetchScalarGridSpec(
            num_scalar_prefetch=2,
            grid=(1,),
            in_specs=[pl.BlockSpec((depth, columns), lambda g, slot, mask: (slot[0], 0))],
            out_specs=pl.BlockSpec((depth, columns), lambda g, slot, mask: (0, 0)),
        ),
        out_shape=jax.ShapeDtypeStruct((depth, columns), mat_b.dtype),
        compiler_params=pltpu.CompilerParams(vmem_limit_bytes=VMEM),
        name="pick_b",
    )(slot, mask_b, mat_b)


def mask_rows(mask_ref, a_ref, held, first_block):
    for r in range(a_ref.shape[0] // BLK):
        for k in range(a_ref.shape[1] // BLK):
            rows, cols = pl.ds(r * BLK, BLK), pl.ds(k * BLK, BLK)
            held[rows, cols] = masked(a_ref[rows, cols], mask_ref[first_block + r, k])


def own_kernel(mask_a_ref, mask_b_ref, a_ref, b_ref, out_ref, held_a, held_b):
    step = pl.program_id(0)

    @pl.when(step == 0)
    def _():
        for k in range(b_ref.shape[0] // BLK):
            for c in range(b_ref.shape[1] // BLK):
                rows, cols = pl.ds(k * BLK, BLK), pl.ds(c * BLK, BLK)
                held_b[rows, cols] = masked(b_ref[rows, cols], mask_b_ref[k, c])

    mask_rows(mask_a_ref, a_ref, held_a, step * STEP_BLOCKS)
    out_ref[...] = jnp.dot(held_a[...], held_b[...], preferred_element_type=jnp.float32)


def own_product(mat_a, mat_b, mask_a, mask_b):
    rows, depth = mat_a.shape
    columns = mat_b.shape[1]
    height = STEP_BLOCKS * BLK
    return pl.pallas_call(
        own_kernel,
        grid_spec=pltpu.PrefetchScalarGridSpec(
            num_scalar_prefetch=2,
            grid=(rows // height,),
            in_specs=[
                pl.BlockSpec((height, depth), lambda g, ma, mb: (g, 0)),
                pl.BlockSpec((depth, columns), lambda g, ma, mb: (0, 0)),
            ],
            out_specs=pl.BlockSpec((height, columns), lambda g, ma, mb: (g, 0)),
            scratch_shapes=[
                pltpu.VMEM((height, depth), mat_a.dtype),
                pltpu.VMEM((depth, columns), mat_b.dtype),
            ],
        ),
        out_shape=jax.ShapeDtypeStruct((rows, columns), jnp.float32),
        compiler_params=pltpu.CompilerParams(vmem_limit_bytes=VMEM),
        cost_estimate=pl.CostEstimate(
            flops=2 * rows * depth * columns, bytes_accessed=2 * rows * depth + 4 * rows * columns, transcendentals=0
        ),
        name="own_product",
    )(mask_a, mask_b, mat_a, mat_b)


def away_kernel(mask_a_ref, a_ref, b_ref, out_ref, held_a, *, first):
    step = pl.program_id(0)
    mask_rows(mask_a_ref, a_ref, held_a, (first + step) * STEP_BLOCKS)
    product = jnp.dot(held_a[...], b_ref[...], preferred_element_type=jnp.float32)
    place = lax.broadcasted_iota(jnp.int32, (PAD, product.shape[1]), 0)
    powers = jnp.zeros(place.shape, jnp.float32)
    for r in range(STEP_BLOCKS):
        piece = product[r * BLK : (r + 1) * BLK]
        most = jnp.max(jnp.max(jnp.abs(piece), axis=0, keepdims=True), axis=1, keepdims=True)
        power = jnp.ceil(jnp.log2(jnp.maximum(most, 1e-30)) + 0.01)
        coded = jnp.round(piece * (32767.0 * jnp.exp2(-power)))
        coded = jnp.clip(coded, -32767.0, 32767.0)
        out_ref[r * BLK : (r + 1) * BLK] = coded.astype(jnp.int32).astype(jnp.int16)
        powers = jnp.where(place == r, power, powers)
    out_ref[STEP_BLOCKS * BLK :] = powers.astype(jnp.int32).astype(jnp.int16)


def away_product(mat_a, right, mask_a, first, steps):
    depth = mat_a.shape[1]
    columns = right.shape[1]
    height = STEP_BLOCKS * BLK
    return pl.pallas_call(
        functools.partial(away_kernel, first=first),
        grid_spec=pltpu.PrefetchScalarGridSpec(
            num_scalar_prefetch=1,
            grid=(steps,),
            in_specs=[
                pl.BlockSpec((height, depth), lambda g, ma: (first + g, 0)),
                pl.BlockSpec((depth, columns), lambda g, ma: (0, 0)),
            ],
            out_specs=pl.BlockSpec((height + PAD, columns), lambda g, ma: (g, 0)),
            scratch_shapes=[pltpu.VMEM((height, depth), mat_a.dtype)],
        ),
        out_shape=jax.ShapeDtypeStruct((steps * (height + PAD), columns), jnp.int16),
        compiler_params=pltpu.CompilerParams(vmem_limit_bytes=VMEM),
        cost_estimate=pl.CostEstimate(
            flops=2 * steps * height * depth * columns, bytes_accessed=2 * steps * height * depth, transcendentals=0
        ),
        name="away_product",
    )(mask_a, mat_a, right)


def join_kernel(first_ref, coded_ref, *rest):
    out_ref = rest[-1]
    powers = coded_ref[STEP_BLOCKS * BLK :].astype(jnp.int32).astype(jnp.float32)
    for r in range(STEP_BLOCKS):
        rows = slice(r * BLK, (r + 1) * BLK)
        scale = jnp.exp2(powers[r : r + 1]) * (1.0 / 32767.0)
        far = coded_ref[rows].astype(jnp.int32).astype(jnp.float32) * scale
        out_ref[rows] = (first_ref[rows] + far).astype(jnp.bfloat16)


def join(own, coded, held, first, steps):
    rows, columns = own.shape
    height = STEP_BLOCKS * BLK
    specs = [
        pl.BlockSpec((height, columns), lambda g: (first + g, 0)),
        pl.BlockSpec((height + PAD, columns), lambda g: (g, 0)),
    ]
    operands = [own, coded]
    aliases = {}
    if held is not None:
        specs.append(pl.BlockSpec(memory_space=pl.ANY))
        operands.append(held)
        aliases = {2: 0}
    return pl.pallas_call(
        join_kernel,
        grid=(steps,),
        in_specs=specs,
        out_specs=pl.BlockSpec((height, columns), lambda g: (first + g, 0)),
        out_shape=jax.ShapeDtypeStruct((rows, columns), jnp.bfloat16),
        input_output_aliases=aliases,
        compiler_params=pltpu.CompilerParams(vmem_limit_bytes=VMEM),
        cost_estimate=pl.CostEstimate(
            flops=2 * steps * height * columns, bytes_accessed=8 * steps * height * columns, transcendentals=0
        ),
        name="join",
    )(*operands)


def body(mat_a, mat_b, mask_a, mask_b):
    depth = mat_a.shape[1]
    n_row, n_col = lax.axis_size("row"), lax.axis_size("col")
    slot = jnp.where(lax.axis_index("row") == 0, 1, 0).astype(jnp.int32)[None]
    give_b = [
        (i * n_col + j, ((i - 1) % n_row) * n_col + (j + 1) % n_col) for i in range(n_row) for j in range(n_col)
    ]
    give_c = [(i * n_col + j, i * n_col + (j - 1) % n_col) for i in range(n_row) for j in range(n_col)]
    right = lax.ppermute(pick_b(mat_b, mask_b, slot, depth), ("row", "col"), give_b)
    own = own_product(mat_a, mat_b, mask_a, mask_b)
    steps = mat_a.shape[0] // (STEP_BLOCKS * BLK) // HALVES
    arrived = []
    for half in range(HALVES):
        coded = away_product(mat_a, right, mask_a, half * steps, steps)
        arrived.append(lax.ppermute(coded, ("row", "col"), give_c))
    out = None
    for half in range(HALVES):
        out = join(own, arrived[half], out, half * steps, steps)
    return out


def solution(mesh):
    return jax.shard_map(
        body,
        mesh=mesh,
        in_specs=(P("row", "col"), P("row", "col"), P("row", "col"), P("row", "col")),
        out_specs=P("row", "col"),
        check_vma=False,
    )
```

time: 423 us -> 119 us (0.28)
  the two profiles are of different devices: /device:TPU:0 before, /device:TPU:71 now
where the time goes in v1:
time: 119 us
  waiting for transfers between devices  76 us (64%)
  Pallas kernels  26.5 us (22%)
  starting transfers between devices  11.5 us (10%)
  local copies, waits for them, and re-layouts  4.67 us (4%)
    ppermute x1, waiting for transfers between devices, body(): lax.ppermute(pick_b(mat_b, mask_b, slot, depth), ('row', 'col'), give_b)  45.3 us
    ppermute x2, waiting for transfers between devices, body(): arrived.append(lax.ppermute(coded, ('row', 'col'), give_c))  30.8 us
    pallas_call x2, Pallas kernels, away_product(): pl.pallas_call(functools.partial(away_kernel, first=first), grid_spec=plt...  10.3 us
    pallas_call x1, Pallas kernels, own_product(): pl.pallas_call(own_kernel, grid_spec=pltpu.PrefetchScalarGridSpec(num_sca...  8.32 us
    ppermute x2, starting transfers between devices, body(): arrived.append(lax.ppermute(coded, ('row', 'col'), give_c))  5.8 us
    ppermute x1, starting transfers between devices, body(): lax.ppermute(pick_b(mat_b, mask_b, slot, depth), ('row', 'col'), give_b)  5.67 us
    unnamed x10, local copies, waits for them, and re-layouts  4.67 us
    pallas_call x2, Pallas kernels, join(): pl.pallas_call(join_kernel, grid=(steps,), in_specs=specs, out_specs=pl.B...  4.6 us
  transfers between devices with their start and end apart: 3, of which 3 were waited for; matrix products, arithmetic and copies ran while one was open for 1% of the time, Pallas kernels for 13%

profile of v1, /device:TPU:71, one launch (start us, length us, event | category | flops | bytes accessed | tf_op | source)
XLA Modules:
  0.0 118.7 jit_solution(12515852290828685646)
XLA Ops:
  0.0 0.0 copy-start.3
  0.0 1.4 %copy.7.mask_b_ref.mask_ref = s32[48,2]{1,0:T(8,128)} copy(s32[48,2]{0,1:T(2,128)} %param.7) | data formatting | bytes 768 | tf_op args[3]
  1.4 3.3 %pick_b.1 = bf16[1536,256]{1,0:T(8,128)(2,1)} custom-call(s32[1]{0:T(128)} %bitcast.slot_ref, s32[48,2]{1,0:T(8,128)} %copy.7.mask_b_ref.mask_ref, bf16[6144,256]{1,0:T(8,128)(2,1)} %b_ref.3), custom_call_target="tpu_custom_call" | custom-call | tf_op jit(solution)/shard_map/pick_b/pallas_call | solution.py:31
  4.6 5.7 %collective-permute-start = (bf16[1536,256]{1,0:T(8,128)(2,1)}, bf16[1536,256]{1,0:T(8,128)(2,1)S(1)}, u32[]{:S(2)}, u32[]{:S(2)}) collective-permute-start(bf16[1536,256]{1,0:T(8,128)(2,1)} %pick_b.1), channel_id=1, source_target_pairs={{0,225},{1,226},{2,227},{3,228},{4,229},{5,230},{6,231},{7,232},{8... | collective-permute-start | bytes 2359304 | tf_op jit(solution)/shard_map/ppermute | solution.py:182
  10.3 0.0 copy-done.3
  10.3 0.7 copy.6.mask_a_ref
  11.0 45.3 %collective-permute-done.b_ref = bf16[1536,256]{1,0:T(8,128)(2,1)S(1)} collective-permute-done((bf16[1536,256]{1,0:T(8,128)(2,1)}, bf16[1536,256]{1,0:T(8,128)(2,1)S(1)}, u32[]{:S(2)}, u32[]{:S(2)}) %collective-permute-start) | collective-permute-done | bytes 786464 | tf_op jit(solution)/shard_map/ppermute | solution.py:182
  56.3 0.0 copy-start
  56.3 0.9 copy-done
  57.2 5.1 %away_product.3 = s16[1312,256]{1,0:T(8,128)(2,1)} custom-call(s32[20,12]{1,0:T(8,128)} %copy.6.mask_a_ref, bf16[2560,1536]{1,0:T(8,128)(2,1)} %a_ref.5, bf16[1536,256]{1,0:T(8,128)(2,1)} %copy-done), custom_call_target="tpu_custom_call" | custom-call | flops 1006632960 | bytes 3932160 | tf_op jit(solution)/shard_map/away_product/pallas_call | solution.py:115
  62.3 4.6 %collective-permute-start.2 = (s16[1312,256]{1,0:T(8,128)(2,1)}, s16[1312,256]{1,0:T(8,128)(2,1)S(1)}, u32[]{:S(2)}, u32[]{:S(2)}) collective-permute-start(s16[1312,256]{1,0:T(8,128)(2,1)} %away_product.3), channel_id=1, source_target_pairs={{0,31},{1,0},{2,1},{3,2},{4,3},{5,4},{6,5},{7,6},{8,7},{9,8},{10,9... | collective-permute-start | bytes 2015240 | tf_op jit(solution)/shard_map/ppermute | solution.py:188
  66.9 5.2 %away_product.2 = s16[1312,256]{1,0:T(8,128)(2,1)} custom-call(s32[20,12]{1,0:T(8,128)} %copy.6.mask_a_ref, bf16[2560,1536]{1,0:T(8,128)(2,1)} %a_ref.5, bf16[1536,256]{1,0:T(8,128)(2,1)} %copy-done), custom_call_target="tpu_custom_call" | custom-call | flops 1006632960 | bytes 3932160 | tf_op jit(solution)/shard_map/away_product/pallas_call | solution.py:115
  72.1 1.2 collective-permute-start.1
  73.3 8.3 %own_product.1.first_ref = f32[2560,256]{1,0:T(8,128)} custom-call(s32[20,12]{1,0:T(8,128)} %copy.6.mask_a_ref, s32[48,2]{1,0:T(8,128)} %copy.7.mask_b_ref.mask_ref, bf16[2560,1536]{1,0:T(8,128)(2,1)} %a_ref.5, bf16[6144,256]{1,0:T(8,128)(2,1)} %b_ref.3), custom_call_target="tpu_custom_call" | custom-call | flops 2013265920 | bytes 10485760 | tf_op jit(solution)/shard_map/own_product/pallas_call | solution.py:70
  81.6 19.8 %collective-permute-done.2.coded_ref = s16[1312,256]{1,0:T(8,128)(2,1)S(1)} collective-permute-done((s16[1312,256]{1,0:T(8,128)(2,1)}, s16[1312,256]{1,0:T(8,128)(2,1)S(1)}, u32[]{:S(2)}, u32[]{:S(2)}) %collective-permute-start.2) | collective-permute-done | bytes 671776 | tf_op jit(solution)/shard_map/ppermute | solution.py:188
  101.4 0.0 copy-start.1
  101.4 0.9 copy-done.1
  102.3 2.3 %join.2.rest_0_ = bf16[2560,256]{1,0:T(8,128)(2,1)} custom-call(f32[2560,256]{1,0:T(8,128)} %own_product.1.first_ref, s16[1312,256]{1,0:T(8,128)(2,1)} %copy-done.1), custom_call_target="tpu_custom_call" | custom-call | flops 655360 | bytes 2621440 | tf_op jit(solution)/shard_map/join/pallas_call | solution.py:159
  104.6 11.0 %collective-permute-done.1.coded_ref = s16[1312,256]{1,0:T(8,128)(2,1)S(1)} collective-permute-done((s16[1312,256]{1,0:T(8,128)(2,1)}, s16[1312,256]{1,0:T(8,128)(2,1)S(1)}, u32[]{:S(2)}, u32[]{:S(2)}) %collective-permute-start.1) | collective-permute-done | bytes 671776 | tf_op jit(solution)/shard_map/ppermute | solution.py:188
  115.5 0.0 copy-start.2
  115.5 0.9 copy-done.2
  116.4 2.3 %join.3 = bf16[2560,256]{1,0:T(8,128)(2,1)} custom-call(f32[2560,256]{1,0:T(8,128)} %own_product.1.first_ref, s16[1312,256]{1,0:T(8,128)(2,1)} %copy-done.2, bf16[2560,256]{1,0:T(8,128)(2,1)} %join.2.rest_0_), custom_call_target="tpu_custom_call", output_to_operand_aliasing={{}: (2, {})} | custom-call | flops 655360 | bytes 2621440 | tf_op jit(solution)/shard_map/join/pallas_call | solution.py:159
Async XLA Ops:
  0.0 10.3 %copy-start.3 = (s32[20,12]{0,1:T(8,128)S(1)}, s32[20,12]{0,1:T(8,128)}, u32[]{:S(2)}) copy-start(s32[20,12]{0,1:T(8,128)} %param.6) | copy-start | bytes 2884
  4.6 51.6 %collective-permute-start = (bf16[1536,256]{1,0:T(8,128)(2,1)}, bf16[1536,256]{1,0:T(8,128)(2,1)S(1)}, u32[]{:S(2)}, u32[]{:S(2)}) collective-permute-start(bf16[1536,256]{1,0:T(8,128)(2,1)} %pick_b.1), channel_id=1, source_target_pairs={{0,225},{1,226},{2,227},{3,228},{4,229},{5,230},{6,231},{7,232},{8... | collective-permute-start | bytes 2359304 | tf_op jit(solution)/shard_map/ppermute | solution.py:182
  56.3 0.9 copy-start
  62.3 39.1 %collective-permute-start.2 = (s16[1312,256]{1,0:T(8,128)(2,1)}, s16[1312,256]{1,0:T(8,128)(2,1)S(1)}, u32[]{:S(2)}, u32[]{:S(2)}) collective-permute-start(s16[1312,256]{1,0:T(8,128)(2,1)} %away_product.3), channel_id=1, source_target_pairs={{0,31},{1,0},{2,1},{3,2},{4,3},{5,4},{6,5},{7,6},{8,7},{9,8},{10,9... | collective-permute-start | bytes 2015240 | tf_op jit(solution)/shard_map/ppermute | solution.py:188
  72.1 43.4 %collective-permute-start.1 = (s16[1312,256]{1,0:T(8,128)(2,1)}, s16[1312,256]{1,0:T(8,128)(2,1)S(1)}, u32[]{:S(2)}, u32[]{:S(2)}) collective-permute-start(s16[1312,256]{1,0:T(8,128)(2,1)} %away_product.2), channel_id=1, source_target_pairs={{0,31},{1,0},{2,1},{3,2},{4,3},{5,4},{6,5},{7,6},{8,7},{9,8},{10,9... | collective-permute-start | bytes 2015240 | tf_op jit(solution)/shard_map/ppermute | solution.py:188
  101.4 0.9 copy-start.1
  115.5 0.9 copy-start.2

commit v2 on v1

v2 whole, which is shorter than its diff:
```python
import functools

import jax
import jax.numpy as jnp
from jax import lax
from jax.experimental import pallas as pl
from jax.experimental.pallas import tpu as pltpu
from jax.sharding import PartitionSpec as P

BLK = 128
STEP_BLOCKS = 5
PAD = 16
JOIN_BLOCKS = 5
PARTS = 2
MIB = 1024 * 1024


def masked(block, flag):
    return jnp.where(flag > 0, block, jnp.zeros_like(block))


def pick_kernel(place_ref, mask_ref, *refs):
    for which in range(2):
        b_ref, out_ref = refs[which], refs[2 + which]
        blocks = b_ref.shape[0] // BLK
        base = place_ref[which] * blocks
        for k in range(blocks):
            for c in range(b_ref.shape[1] // BLK):
                rows, cols = pl.ds(k * BLK, BLK), pl.ds(c * BLK, BLK)
                out_ref[rows, cols] = masked(b_ref[rows, cols], mask_ref[c, base + k])


def pick_b(mat_b, mask_b, places, half):
    columns = mat_b.shape[1]
    return pl.pallas_call(
        pick_kernel,
        grid_spec=pltpu.PrefetchScalarGridSpec(
            num_scalar_prefetch=2,
            grid=(1,),
            in_specs=[
                pl.BlockSpec((half, columns), lambda g, places, mask: (places[0], 0)),
                pl.BlockSpec((half, columns), lambda g, places, mask: (places[1], 0)),
            ],
            out_specs=[pl.BlockSpec((half, columns), lambda g, places, mask: (0, 0))] * 2,
        ),
        out_shape=[jax.ShapeDtypeStruct((half, columns), mat_b.dtype)] * 2,
        compiler_params=pltpu.CompilerParams(vmem_limit_bytes=60 * MIB),
        name="pick_b",
    )(places, mask_b.T, mat_b, mat_b)


def mask_rows(mask_ref, a_ref, held, first_block):
    for r in range(a_ref.shape[0] // BLK):
        for k in range(a_ref.shape[1] // BLK):
            rows, cols = pl.ds(r * BLK, BLK), pl.ds(k * BLK, BLK)
            held[rows, cols] = masked(a_ref[rows, cols], mask_ref[k, first_block + r])


def own_kernel(mask_a_ref, mask_b_ref, a_ref, b_ref, out_ref, held_a, held_b):
    step = pl.program_id(0)

    @pl.when(step == 0)
    def _():
        for k in range(b_ref.shape[0] // BLK):
            for c in range(b_ref.shape[1] // BLK):
                rows, cols = pl.ds(k * BLK, BLK), pl.ds(c * BLK, BLK)
                held_b[rows, cols] = masked(b_ref[rows, cols], mask_b_ref[c, k])

    mask_rows(mask_a_ref, a_ref, held_a, step * STEP_BLOCKS)
    out_ref[...] = jnp.dot(held_a[...], held_b[...], preferred_element_type=jnp.float32)


def own_product(mat_a, mat_b, mask_a, mask_b):
    rows, depth = mat_a.shape
    columns = mat_b.shape[1]
    height = STEP_BLOCKS * BLK
    return pl.pallas_call(
        own_kernel,
        grid_spec=pltpu.PrefetchScalarGridSpec(
            num_scalar_prefetch=2,
            grid=(rows // height,),
            in_specs=[
                pl.BlockSpec((height, depth), lambda g, ma, mb: (g, 0)),
                pl.BlockSpec((depth, columns), lambda g, ma, mb: (0, 0)),
            ],
            out_specs=[
                pl.BlockSpec((height, columns), lambda g, ma, mb: (g, 0)),
                pl.BlockSpec((height, depth), lambda g, ma, mb: (g, 0)),
            ],
            scratch_shapes=[pltpu.VMEM((depth, columns), mat_b.dtype)],
        ),
        out_shape=[
            jax.ShapeDtypeStruct((rows, columns), jnp.float32),
            jax.ShapeDtypeStruct((rows, depth), mat_a.dtype),
        ],
        compiler_params=pltpu.CompilerParams(vmem_limit_bytes=24 * MIB),
        cost_estimate=pl.CostEstimate(
            flops=2 * rows * depth * columns, bytes_accessed=4 * rows * depth + 4 * rows * columns, transcendentals=0
        ),
        name="own_product",
    )(mask_a.T, mask_b.T, mat_a, mat_b)


def away_kernel(core_ref, a_ref, once_ref, twice_ref, relayed_ref, out_ref):
    rows, columns = a_ref.shape[0], out_ref.shape[1]
    half = once_ref.shape[0]
    height = STEP_BLOCKS * BLK

    def multiply(top_ref, bottom_ref):
        powers = []
        for first in range(0, rows, height):
            here = slice(first, first + height)
            product = jnp.dot(a_ref[here, :half], top_ref[...], preferred_element_type=jnp.float32)
            product += jnp.dot(a_ref[here, half:], bottom_ref[...], preferred_element_type=jnp.float32)
            pieces = product.reshape(STEP_BLOCKS, BLK, columns)
            most = jnp.max(jnp.max(jnp.abs(pieces), axis=1), axis=1, keepdims=True)
            power = jnp.ceil(jnp.log2(jnp.maximum(most, 1e-30)) + 0.01)
            scale = 32767.0 * jnp.exp2(-power)
            coded = jnp.round(pieces * scale[:, :, None])
            coded = jnp.clip(coded, -32767.0, 32767.0).reshape(height, columns)
            out_ref[here] = coded.astype(jnp.int32).astype(jnp.int16)
            powers.append(jnp.broadcast_to(power, (STEP_BLOCKS, columns)))
        powers.append(jnp.zeros((PAD - rows // BLK, columns), jnp.float32))
        out_ref[rows:] = jnp.concatenate(powers, axis=0).astype(jnp.int32).astype(jnp.int16)

    @pl.when(core_ref[0] == 0)
    def _():
        multiply(relayed_ref, twice_ref)

    @pl.when(core_ref[0] == 1)
    def _():
        multiply(twice_ref, once_ref)


def away_product(held_a, rights, core, part):
    rows, depth = held_a.shape[0] // PARTS, held_a.shape[1]
    columns = rights[0].shape[1]
    return pl.pallas_call(
        away_kernel,
        grid=(1,),
        in_specs=[pl.BlockSpec(memory_space=pltpu.SMEM), pl.BlockSpec((rows, depth), lambda g: (part, 0))]
        + [pl.BlockSpec(memory_space=pltpu.VMEM)] * len(rights),
        out_specs=pl.BlockSpec((rows + PAD, columns), lambda g: (0, 0)),
        out_shape=jax.ShapeDtypeStruct((rows + PAD, columns), jnp.int16),
        compiler_params=pltpu.CompilerParams(vmem_limit_bytes=24 * MIB),
        cost_estimate=pl.CostEstimate(
            flops=2 * rows * depth * columns, bytes_accessed=2 * rows * depth, transcendentals=0
        ),
        name="away_product",
    )(core, held_a, *rights)


def join_kernel(own_ref, coded_ref, *rest):
    out_ref, scales = rest[-2:]
    rows = coded_ref.shape[0] - PAD
    scales[...] = jnp.exp2(coded_ref[rows:].astype(jnp.int32).astype(jnp.float32)) * (1.0 / 32767.0)
    first = pl.program_id(0) * JOIN_BLOCKS
    for r in range(JOIN_BLOCKS):
        here = slice(r * BLK, (r + 1) * BLK)
        scale = scales[pl.ds(first + r, 1)]
        far = coded_ref[pl.ds(pl.multiple_of((first + r) * BLK, BLK), BLK)].astype(jnp.int32).astype(jnp.float32) * scale
        out_ref[here] = (own_ref[here] + far).astype(jnp.bfloat16)


def join(own, coded, held, part):
    columns = own.shape[1]
    height = JOIN_BLOCKS * BLK
    steps = own.shape[0] // PARTS // height
    specs = [
        pl.BlockSpec((height, columns), lambda g: (part * steps + g, 0)),
        pl.BlockSpec(memory_space=pltpu.VMEM),
    ]
    operands = [own, coded]
    aliases = {}
    if held is not None:
        specs.append(pl.BlockSpec(memory_space=pl.ANY))
        operands.append(held)
        aliases = {2: 0}
    return pl.pallas_call(
        join_kernel,
        grid=(steps,),
        in_specs=specs,
        out_specs=pl.BlockSpec((height, columns), lambda g: (part * steps + g, 0)),
        out_shape=jax.ShapeDtypeStruct(own.shape, jnp.bfloat16),
        scratch_shapes=[pltpu.VMEM((PAD, columns), jnp.float32)],
        input_output_aliases=aliases,
        compiler_params=pltpu.CompilerParams(vmem_limit_bytes=24 * MIB),
        cost_estimate=pl.CostEstimate(
            flops=2 * steps * height * columns, bytes_accessed=8 * steps * height * columns, transcendentals=0
        ),
        name="join",
    )(*operands)


def routes(n_row, n_col):
    def place(device):
        i, j = divmod(device, n_col)
        return j // 2, (j % 2) * (n_row // 2) + i // 2, i % 2

    def at(plane, z, core):
        half, low = divmod(z % n_row, n_row // 2)
        return (low * 2 + core) * n_col + plane * 2 + half

    devices = range(n_row * n_col)
    give_b = [(d, ((d // n_col - 1) % n_row) * n_col + (d % n_col + 1) % n_col) for d in devices]
    give_c = [(d, d // n_col * n_col + (d % n_col - 1) % n_col) for d in devices]
    first_leg, second_leg = [], []
    for source, target in give_b:
        plane, z, core = place(target)
        if core == 1:
            first_leg.append((source, target))
        else:
            middle = at(plane, z + 2, core)
            first_leg.append((source, middle))
            second_leg.append((middle, target))
    return give_b, first_leg, second_leg, give_c


def body(mat_a, mat_b, mask_a, mask_b):
    depth = mat_a.shape[1]
    axes = ("row", "col")
    give_b, first_leg, second_leg, give_c = routes(lax.axis_size("row"), lax.axis_size("col"))
    place = lax.axis_index("row")
    slot = jnp.where(place == 0, 1, 0).astype(jnp.int32)
    core = lax.rem(place, 2).astype(jnp.int32)
    places = jnp.stack([2 * slot + 1 - core, 2 * slot + core])
    once, twice = pick_b(mat_b, mask_b, places, depth // 2)
    once = lax.ppermute(once, axes, first_leg)
    twice = lax.ppermute(twice, axes, give_b)
    relayed = lax.ppermute(once, axes, second_leg)
    own, held_a = own_product(mat_a, mat_b, mask_a, mask_b)
    arrived = []
    for part in range(PARTS):
        coded = away_product(held_a, [once, twice, relayed], core[None], part)
        arrived.append(lax.ppermute(coded, axes, give_c))
    out = None
    for part in range(PARTS):
        out = join(own, arrived[part], out, part)
    return out


def solution(mesh):
    return jax.shard_map(
        body,
        mesh=mesh,
        in_specs=(P("row", "col"), P("row", "col"), P("row", "col"), P("row", "col")),
        out_specs=P("row", "col"),
        check_vma=False,
    )
```

time: 119 us -> 112 us (0.941)
  the two profiles are of different devices: /device:TPU:71 before, /device:TPU:96 now
where the time goes in v2:
time: 112 us; the launch traced here: 111 us
  waiting for transfers between devices  78.6 us (70%)
  starting transfers between devices  16.7 us (15%)
  Pallas kernels  12.2 us (11%)
  local copies, waits for them, and re-layouts  3.24 us (3%)
    ppermute x2, waiting for transfers between devices, body(): arrived.append(lax.ppermute(coded, axes, give_c))  33.5 us
    ppermute x1, waiting for transfers between devices, body(): once = lax.ppermute(once, axes, first_leg)  28.1 us
    ppermute x1, waiting for transfers between devices, body(): relayed = lax.ppermute(once, axes, second_leg)  17 us
    ppermute x2, starting transfers between devices, body(): arrived.append(lax.ppermute(coded, axes, give_c))  8.57 us
    pallas_call x1, Pallas kernels, own_product(): pl.pallas_call(own_kernel, grid_spec=pltpu.PrefetchScalarGridSpec(num_sca...  4.05 us
    ppermute x1, starting transfers between devices, body(): once = lax.ppermute(once, axes, first_leg)  3.48 us
    unnamed x8, local copies, waits for them, and re-layouts  3.24 us
    pallas_call x1, Pallas kernels, pick_b(): pl.pallas_call(pick_kernel, grid_spec=pltpu.PrefetchScalarGridSpec(num_sc...  3.14 us
  transfers between devices with their start and end apart: 5, of which 4 were waited for; matrix products, arithmetic and copies ran while one was open for 0% of the time, Pallas kernels for 6%

profile of v2, /device:TPU:96, one launch (start us, length us, event | category | flops | bytes accessed | tf_op | source)
XLA Modules:
  0.0 111.4 jit_solution(18384446503761894188)
XLA Ops:
  0.0 0.6 pad_add_fusion.place_ref
  0.6 0.0 copy-start
  0.6 0.0 copy-start.2
  0.6 3.1 %pick_b.1 = (bf16[768,256]{1,0:T(8,128)(2,1)}, bf16[768,256]{1,0:T(8,128)(2,1)}) custom-call(s32[2]{0:T(128)} %pad_add_fusion.place_ref, s32[2,48]{1,0:T(2,128)} %bitcast.6, bf16[6144,256]{1,0:T(8,128)(2,1)} %refs_1_.1, bf16[6144,256]{1,0:T(8,128)(2,1)} %refs_1_.1), custom_call_target="tpu_custom_call" | custom-call | tf_op jit(solution)/shard_map/pick_b/pallas_call | solution.py:35
  3.7 3.5 %collective-permute-start = (bf16[768,256]{1,0:T(8,128)(2,1)}, bf16[768,256]{1,0:T(8,128)(2,1)S(1)}, u32[]{:S(2)}, u32[]{:S(2)}) collective-permute-start(bf16[768,256]{1,0:T(8,128)(2,1)} %get-tuple-element.11), channel_id=1, source_target_pairs={{0,225},{1,226},{2,227},{3,228},{4,229},{5,230},{6,231},{7,232},{8... | collective-permute-start | bytes 1179656 | tf_op jit(solution)/shard_map/ppermute | solution.py:228
  7.2 2.7 %collective-permute-start.1 = (bf16[768,256]{1,0:T(8,128)(2,1)}, bf16[768,256]{1,0:T(8,128)(2,1)S(1)}, u32[]{:S(2)}, u32[]{:S(2)}) collective-permute-start(bf16[768,256]{1,0:T(8,128)(2,1)} %get-tuple-element.12), channel_id=1, source_target_pairs={{0,225},{1,226},{2,227},{3,228},{4,229},{5,230},{6,231},{7,232},{8... | collective-permute-start | bytes 1179656 | tf_op jit(solution)/shard_map/ppermute | solution.py:229
  9.9 28.1 %collective-permute-done.once_ref = bf16[768,256]{1,0:T(8,128)(2,1)S(1)} collective-permute-done((bf16[768,256]{1,0:T(8,128)(2,1)}, bf16[768,256]{1,0:T(8,128)(2,1)S(1)}, u32[]{:S(2)}, u32[]{:S(2)}) %collective-permute-start) | collective-permute-done | bytes 393248 | tf_op jit(solution)/shard_map/ppermute | solution.py:228
  38.1 1.9 %collective-permute-start.2 = (bf16[768,256]{1,0:T(8,128)(2,1)S(1)}, bf16[768,256]{1,0:T(8,128)(2,1)S(1)}, u32[]{:S(2)}, u32[]{:S(2)}) collective-permute-start(bf16[768,256]{1,0:T(8,128)(2,1)S(1)} %collective-permute-done.once_ref), channel_id=1, source_target_pairs={{129,1},{130,2},{131,3},{132,4},{133,5},{134,6},{135,7},{136,8},{1... | collective-permute-start | bytes 1179656 | tf_op jit(solution)/shard_map/ppermute | solution.py:230
  40.0 0.0 copy-done
  40.0 0.0 copy-done.2
  40.0 0.0 copy-done.3
  40.0 0.0 copy-start.1
  40.1 3.2 %copy-done.1 = bf16[2560,1536]{1,0:T(8,128)(2,1)S(1)} copy-done((bf16[2560,1536]{1,0:T(8,128)(2,1)S(1)}, bf16[2560,1536]{1,0:T(8,128)(2,1)}, u32[]{:S(2)}) %copy-start.1) | copy-done | bytes 7864344
  43.3 4.0 %own_product.1 = (f32[2560,256]{1,0:T(8,128)S(1)}, bf16[2560,1536]{1,0:T(8,128)(2,1)S(1)}) custom-call(s32[12,20]{1,0:T(8,128)S(1)} %bitcast.5, s32[2,48]{1,0:T(2,128)S(1)} %bitcast.7, bf16[2560,1536]{1,0:T(8,128)(2,1)S(1)} %copy-done.1, bf16[6144,256]{1,0:T(8,128)(2,1)S(1)} %copy-done), custom_call_target="tpu_custom_call" | custom-call | flops 2013265920 | bytes 18350080 | tf_op jit(solution)/shard_map/own_product/pallas_call | solution.py:77
  47.3 0.0 collective-permute-done.1.twice_ref
  47.3 17.0 %collective-permute-done.2.relayed_ref = bf16[768,256]{1,0:T(8,128)(2,1)S(1)} collective-permute-done((bf16[768,256]{1,0:T(8,128)(2,1)S(1)}, bf16[768,256]{1,0:T(8,128)(2,1)S(1)}, u32[]{:S(2)}, u32[]{:S(2)}) %collective-permute-start.2) | collective-permute-done | bytes 393248 | tf_op jit(solution)/shard_map/ppermute | solution.py:230
  64.3 1.5 %away_product.3 = s16[1296,256]{1,0:T(8,128)(2,1)S(1)} custom-call(s32[1]{0:T(128)} %bitcast.2.core_ref, bf16[2560,1536]{1,0:T(8,128)(2,1)S(1)} %get-tuple-element.10.a_ref, bf16[768,256]{1,0:T(8,128)(2,1)S(1)} %collective-permute-done.once_ref, bf16[768,256]{1,0:T(8,128)(2,1)S(1)} %collective-permute-done.1.twice_ref, ...), custom_call_target="tpu_custom_call" | custom-call | flops 1006632960 | bytes 3932160 | tf_op jit(solution)/shard_map/away_product/pallas_call | solution.py:138
  65.9 0.1 collective-permute-start.4
  65.9 1.6 %away_product.2 = s16[1296,256]{1,0:T(8,128)(2,1)S(1)} custom-call(s32[1]{0:T(128)} %bitcast.2.core_ref, bf16[2560,1536]{1,0:T(8,128)(2,1)S(1)} %get-tuple-element.10.a_ref, bf16[768,256]{1,0:T(8,128)(2,1)S(1)} %collective-permute-done.once_ref, bf16[768,256]{1,0:T(8,128)(2,1)S(1)} %collective-permute-done.1.twice_ref, ...), custom_call_target="tpu_custom_call" | custom-call | flops 1006632960 | bytes 3932160 | tf_op jit(solution)/shard_map/away_product/pallas_call | solution.py:138
  67.5 8.5 %collective-permute-start.3 = (s16[1296,256]{1,0:T(8,128)(2,1)S(1)}, s16[1296,256]{1,0:T(8,128)(2,1)S(1)}, u32[]{:S(2)}, u32[]{:S(2)}) collective-permute-start(s16[1296,256]{1,0:T(8,128)(2,1)S(1)} %away_product.2), channel_id=1, source_target_pairs={{0,31},{1,0},{2,1},{3,2},{4,3},{5,4},{6,5},{7,6},{8,7},{9,8},{10,9... | collective-permute-start | bytes 1990664 | tf_op jit(solution)/shard_map/ppermute | solution.py:235
  76.0 27.3 %collective-permute-done.4.coded_ref = s16[1296,256]{1,0:T(8,128)(2,1)S(1)} collective-permute-done((s16[1296,256]{1,0:T(8,128)(2,1)S(1)}, s16[1296,256]{1,0:T(8,128)(2,1)S(1)}, u32[]{:S(2)}, u32[]{:S(2)}) %collective-permute-start.4) | collective-permute-done | bytes 663584 | tf_op jit(solution)/shard_map/ppermute | solution.py:235
  103.3 1.0 join.2.rest_0_
  104.3 6.2 %collective-permute-done.3.coded_ref = s16[1296,256]{1,0:T(8,128)(2,1)S(1)} collective-permute-done((s16[1296,256]{1,0:T(8,128)(2,1)S(1)}, s16[1296,256]{1,0:T(8,128)(2,1)S(1)}, u32[]{:S(2)}, u32[]{:S(2)}) %collective-permute-start.3) | collective-permute-done | bytes 663584 | tf_op jit(solution)/shard_map/ppermute | solution.py:235
  110.4 1.0 join.3
  (1 shorter events, 0.0 us)
Async XLA Ops:
  0.6 39.4 %copy-start = (bf16[6144,256]{1,0:T(8,128)(2,1)S(1)}, bf16[6144,256]{1,0:T(8,128)(2,1)}, u32[]{:S(2)}) copy-start(bf16[6144,256]{1,0:T(8,128)(2,1)} %refs_1_.1) | copy-start | bytes 9437188
  0.6 39.4 %copy-start.2 = (s32[20,12]{0,1:T(8,128)S(1)}, s32[20,12]{0,1:T(8,128)}, u32[]{:S(2)}) copy-start(s32[20,12]{0,1:T(8,128)} %param.6) | copy-start | bytes 2884
  0.6 39.5 %copy-start.3 = (s32[48,2]{0,1:T(2,128)S(1)}, s32[48,2]{0,1:T(2,128)}, u32[]{:S(2)}) copy-start(s32[48,2]{0,1:T(2,128)} %param.7) | copy-start | bytes 1156
  3.7 34.4 %collective-permute-start = (bf16[768,256]{1,0:T(8,128)(2,1)}, bf16[768,256]{1,0:T(8,128)(2,1)S(1)}, u32[]{:S(2)}, u32[]{:S(2)}) collective-permute-start(bf16[768,256]{1,0:T(8,128)(2,1)} %get-tuple-element.11), channel_id=1, source_target_pairs={{0,225},{1,226},{2,227},{3,228},{4,229},{5,230},{6,231},{7,232},{8... | collective-permute-start | bytes 1179656 | tf_op jit(solution)/shard_map/ppermute | solution.py:228
  7.2 40.1 %collective-permute-start.1 = (bf16[768,256]{1,0:T(8,128)(2,1)}, bf16[768,256]{1,0:T(8,128)(2,1)S(1)}, u32[]{:S(2)}, u32[]{:S(2)}) collective-permute-start(bf16[768,256]{1,0:T(8,128)(2,1)} %get-tuple-element.12), channel_id=1, source_target_pairs={{0,225},{1,226},{2,227},{3,228},{4,229},{5,230},{6,231},{7,232},{8... | collective-permute-start | bytes 1179656 | tf_op jit(solution)/shard_map/ppermute | solution.py:229
  38.1 26.2 %collective-permute-start.2 = (bf16[768,256]{1,0:T(8,128)(2,1)S(1)}, bf16[768,256]{1,0:T(8,128)(2,1)S(1)}, u32[]{:S(2)}, u32[]{:S(2)}) collective-permute-start(bf16[768,256]{1,0:T(8,128)(2,1)S(1)} %collective-permute-done.once_ref), channel_id=1, source_target_pairs={{129,1},{130,2},{131,3},{132,4},{133,5},{134,6},{135,7},{136,8},{1... | collective-permute-start | bytes 1179656 | tf_op jit(solution)/shard_map/ppermute | solution.py:230
  40.0 3.2 %copy-start.1 = (bf16[2560,1536]{1,0:T(8,128)(2,1)S(1)}, bf16[2560,1536]{1,0:T(8,128)(2,1)}, u32[]{:S(2)}) copy-start(bf16[2560,1536]{1,0:T(8,128)(2,1)} %a_ref.1) | copy-start | bytes 23592964
  65.9 37.4 %collective-permute-start.4 = (s16[1296,256]{1,0:T(8,128)(2,1)S(1)}, s16[1296,256]{1,0:T(8,128)(2,1)S(1)}, u32[]{:S(2)}, u32[]{:S(2)}) collective-permute-start(s16[1296,256]{1,0:T(8,128)(2,1)S(1)} %away_product.3), channel_id=1, source_target_pairs={{0,31},{1,0},{2,1},{3,2},{4,3},{5,4},{6,5},{7,6},{8,7},{9,8},{10,9... | collective-permute-start | bytes 1990664 | tf_op jit(solution)/shard_map/ppermute | solution.py:235
  67.5 42.9 %collective-permute-start.3 = (s16[1296,256]{1,0:T(8,128)(2,1)S(1)}, s16[1296,256]{1,0:T(8,128)(2,1)S(1)}, u32[]{:S(2)}, u32[]{:S(2)}) collective-permute-start(s16[1296,256]{1,0:T(8,128)(2,1)S(1)} %away_product.2), channel_id=1, source_target_pairs={{0,31},{1,0},{2,1},{3,2},{4,3},{5,4},{6,5},{7,6},{8,7},{9,8},{10,9... | collective-permute-start | bytes 1990664 | tf_op jit(solution)/shard_map/ppermute | solution.py:235

commit v3 on v2

--- a/solution.py
+++ b/solution.py
@@ -19,34 +19,20 @@
     return jnp.where(flag > 0, block, jnp.zeros_like(block))
 
 
-def pick_kernel(place_ref, mask_ref, *refs):
-    for which in range(2):
-        b_ref, out_ref = refs[which], refs[2 + which]
-        blocks = b_ref.shape[0] // BLK
-        base = place_ref[which] * blocks
-        for k in range(blocks):
-            for c in range(b_ref.shape[1] // BLK):
-                rows, cols = pl.ds(k * BLK, BLK), pl.ds(c * BLK, BLK)
-                out_ref[rows, cols] = masked(b_ref[rows, cols], mask_ref[c, base + k])
-
-
-def pick_b(mat_b, mask_b, places, half):
+def place_of(row, which):
+    slot = jnp.where(row == 0, 1, 0)
+    core = lax.rem(row, 2)
+    return 2 * slot + (1 - core if which == 0 else core)
+
+
+def pick_b(mat_b, mask_b, row, which, half):
     columns = mat_b.shape[1]
-    return pl.pallas_call(
-        pick_kernel,
-        grid_spec=pltpu.PrefetchScalarGridSpec(
-            num_scalar_prefetch=2,
-            grid=(1,),
-            in_specs=[
-                pl.BlockSpec((half, columns), lambda g, places, mask: (places[0], 0)),
-                pl.BlockSpec((half, columns), lambda g, places, mask: (places[1], 0)),
-            ],
-            out_specs=[pl.BlockSpec((half, columns), lambda g, places, mask: (0, 0))] * 2,
-        ),
-        out_shape=[jax.ShapeDtypeStruct((half, columns), mat_b.dtype)] * 2,
-        compiler_params=pltpu.CompilerParams(vmem_limit_bytes=60 * MIB),
-        name="pick_b",
-    )(places, mask_b.T, mat_b, mat_b)
+    blocks = half // BLK
+    place = place_of(row, which)
+    piece = lax.dynamic_slice_in_dim(mat_b, place * half, half, 0)
+    flags = lax.dynamic_slice_in_dim(mask_b, place * blocks, blocks, 0)
+    kept = piece.reshape(blocks, BLK, columns // BLK, BLK) * flags.astype(mat_b.dtype)[:, None, :, None]
+    return kept.reshape(half, columns)
 
 
 def mask_rows(mask_ref, a_ref, held, first_block):
@@ -56,8 +42,9 @@
             held[rows, cols] = masked(a_ref[rows, cols], mask_ref[k, first_block + r])
 
 
-def own_kernel(mask_a_ref, mask_b_ref, a_ref, b_ref, out_ref, held_a, held_b):
+def own_kernel(mask_a_ref, mask_b_ref, a_ref, b_ref, out_ref, held_a, done_ref, held_b):
     step = pl.program_id(0)
+    done_ref[...] = jnp.zeros_like(done_ref)
 
     @pl.when(step == 0)
     def _():
@@ -86,12 +73,14 @@
             out_specs=[
                 pl.BlockSpec((height, columns), lambda g, ma, mb: (g, 0)),
                 pl.BlockSpec((height, depth), lambda g, ma, mb: (g, 0)),
+                pl.BlockSpec((8, BLK), lambda g, ma, mb: (0, 0)),
             ],
             scratch_shapes=[pltpu.VMEM((depth, columns), mat_b.dtype)],
         ),
         out_shape=[
             jax.ShapeDtypeStruct((rows, columns), jnp.float32),
             jax.ShapeDtypeStruct((rows, depth), mat_a.dtype),
+            jax.ShapeDtypeStruct((8, BLK), jnp.float32),
         ],
         compiler_params=pltpu.CompilerParams(vmem_limit_bytes=24 * MIB),
         cost_estimate=pl.CostEstimate(
@@ -99,6 +88,22 @@
         ),
         name="own_product",
     )(mask_a.T, mask_b.T, mat_a, mat_b)
+
+
+def after_kernel(value_ref, done_ref, out_ref):
+    pass
+
+
+def after(value, done):
+    return pl.pallas_call(
+        after_kernel,
+        in_specs=[pl.BlockSpec(memory_space=pl.ANY)] * 2,
+        out_specs=pl.BlockSpec(memory_space=pl.ANY),
+        out_shape=jax.ShapeDtypeStruct(value.shape, value.dtype),
+        input_output_aliases={0: 0},
+        compiler_params=pltpu.CompilerParams(vmem_limit_bytes=MIB),
+        name="after",
+    )(value, done)
 
 
 def away_kernel(core_ref, a_ref, once_ref, twice_ref, relayed_ref, out_ref):
@@ -150,16 +155,17 @@
     )(core, held_a, *rights)
 
 
-def join_kernel(own_ref, coded_ref, *rest):
+def join_kernel(own_ref, coded_ref, *rest, start):
     out_ref, scales = rest[-2:]
     rows = coded_ref.shape[0] - PAD
     scales[...] = jnp.exp2(coded_ref[rows:].astype(jnp.int32).astype(jnp.float32)) * (1.0 / 32767.0)
     first = pl.program_id(0) * JOIN_BLOCKS
     for r in range(JOIN_BLOCKS):
         here = slice(r * BLK, (r + 1) * BLK)
+        there = pl.ds(pl.multiple_of((start + first + r) * BLK, BLK), BLK)
         scale = scales[pl.ds(first + r, 1)]
         far = coded_ref[pl.ds(pl.multiple_of((first + r) * BLK, BLK), BLK)].astype(jnp.int32).astype(jnp.float32) * scale
-        out_ref[here] = (own_ref[here] + far).astype(jnp.bfloat16)
+        out_ref[here] = (own_ref[there] + far).astype(jnp.bfloat16)
 
 
 def join(own, coded, held, part):
@@ -167,7 +173,7 @@
     height = JOIN_BLOCKS * BLK
     steps = own.shape[0] // PARTS // height
     specs = [
-        pl.BlockSpec((height, columns), lambda g: (part * steps + g, 0)),
+        pl.BlockSpec(memory_space=pltpu.VMEM),
         pl.BlockSpec(memory_space=pltpu.VMEM),
     ]
     operands = [own, coded]
@@ -177,7 +183,7 @@
         operands.append(held)
         aliases = {2: 0}
     return pl.pallas_call(
-        join_kernel,
+        functools.partial(join_kernel, start=part * steps * JOIN_BLOCKS),
         grid=(steps,),
         in_specs=specs,
         out_specs=pl.BlockSpec((height, columns), lambda g: (part * steps + g, 0)),
@@ -220,15 +226,13 @@
     depth = mat_a.shape[1]
     axes = ("row", "col")
     give_b, first_leg, second_leg, give_c = routes(lax.axis_size("row"), lax.axis_size("col"))
-    place = lax.axis_index("row")
-    slot = jnp.where(place == 0, 1, 0).astype(jnp.int32)
-    core = lax.rem(place, 2).astype(jnp.int32)
-    places = jnp.stack([2 * slot + 1 - core, 2 * slot + core])
-    once, twice = pick_b(mat_b, mask_b, places, depth // 2)
-    once = lax.ppermute(once, axes, first_leg)
-    twice = lax.ppermute(twice, axes, give_b)
+    place = lax.axis_index("row").astype(jnp.int32)
+    core = lax.rem(place, 2)
+    once = lax.ppermute(pick_b(mat_b, mask_b, place, 0, depth // 2), axes, first_leg)
+    twice = lax.ppermute(pick_b(mat_b, mask_b, place, 1, depth // 2), axes, give_b)
+    own, held_a, done = own_product(mat_a, mat_b, mask_a, mask_b)
+    once = after(once, done)
     relayed = lax.ppermute(once, axes, second_leg)
-    own, held_a = own_product(mat_a, mat_b, mask_a, mask_b)
     arrived = []
     for part in range(PARTS):
         coded = away_product(held_a, [once, twice, relayed], core[None], part)

time: 112 us -> 110 us (0.982)
  the two profiles are of different devices: /device:TPU:96 before, /device:TPU:32 now
where the time goes in v3:
time: 110 us
  waiting for transfers between devices  50.4 us (46%)
  starting transfers between devices  43.9 us (40%)
  Pallas kernels  9.04 us (8%)
  local copies, waits for them, and re-layouts  4 us (4%)
  other arithmetic  2.23 us (2%)
    ppermute x2, waiting for transfers between devices, body(): arrived.append(lax.ppermute(coded, axes, give_c))  34.2 us
    ppermute x1, starting transfers between devices, body(): relayed = lax.ppermute(once, axes, second_leg)  23.6 us
    ppermute x1, waiting for transfers between devices, body(): relayed = lax.ppermute(once, axes, second_leg)  14.8 us
    ppermute x2, starting transfers between devices, body(): arrived.append(lax.ppermute(coded, axes, give_c))  14 us
    ppermute x1, starting transfers between devices, body(): lax.ppermute(pick_b(mat_b, mask_b, place, 0, depth // 2), axes, first_leg)  5.35 us
    pallas_call x1, Pallas kernels, own_product(): pl.pallas_call(own_kernel, grid_spec=pltpu.PrefetchScalarGridSpec(num_sca...  4.04 us
    unnamed x8, local copies, waits for them, and re-layouts  3.24 us
    pallas_call x2, Pallas kernels, away_product(): pl.pallas_call(away_kernel, grid=(1,), in_specs=[pl.BlockSpec(memory_spac...  3.09 us
  transfers between devices with their start and end apart: 5, of which 4 were waited for; matrix products, arithmetic and copies ran while one was open for 0% of the time, Pallas kernels for 6%

profile of v3, /device:TPU:32, one launch (start us, length us, event | category | flops | bytes accessed | tf_op | source)
XLA Modules:
  0.0 109.6 jit_solution(4930764726242175139)
XLA Ops:
  0.0 0.9 dynamic-slice_convert_fusion
  1.0 0.1 copy.8
  1.1 0.1 copy.7
  1.2 0.3 mul.41
  1.5 0.3 mul.46
  1.7 1.3 %bitcast_multiply_fusion = (bf16[768,256]{1,0:T(8,128)(2,1)S(1)}, bf16[768,256]{1,0:T(8,128)(2,1)S(1)}) fusion(bf16[96,8,2,128]{3,2,1,0:T(2,128)(2,1)S(1)} %bitcast.14, bf16[6144,256]{1,0:T(8,128)(2,1)} %b_ref.1, s32[]{:T(128)S(6)} %select_n.20, bf16[96,8,2,128]{3,2,1,0:T(2,128)(2,1)S(1)} %bitcast.13, s32[]{:T(128)S(6)} %select_n.18), kind=kLoop, calls=%fused_computation | loop fusion | flops 1572864 | bytes 2359304 | tf_op jit(solution)/shard_map/mul | solution.py:34
  3.0 5.4 %collective-permute-start = (bf16[768,256]{1,0:T(8,128)(2,1)S(1)}, bf16[768,256]{1,0:T(8,128)(2,1)S(1)}, u32[]{:S(2)}, u32[]{:S(2)}) collective-permute-start(bf16[768,256]{1,0:T(8,128)(2,1)S(1)} %get-tuple-element.12), channel_id=1, source_target_pairs={{0,225},{1,226},{2,227},{3,228},{4,229},{5,230},{6,231},{7,232},{8... | collective-permute-start | bytes 1179656 | tf_op jit(solution)/shard_map/ppermute | solution.py:231
  8.4 0.9 collective-permute-start.1
  9.3 0.0 copy-done.2
  9.3 0.0 copy-done.1
  9.4 3.2 %copy-done = bf16[2560,1536]{1,0:T(8,128)(2,1)S(1)} copy-done((bf16[2560,1536]{1,0:T(8,128)(2,1)S(1)}, bf16[2560,1536]{1,0:T(8,128)(2,1)}, u32[]{:S(2)}) %copy-start) | copy-done | bytes 7864344
  12.6 4.0 %own_product.1 = (f32[2560,256]{1,0:T(8,128)S(1)}, bf16[2560,1536]{1,0:T(8,128)(2,1)S(1)}, f32[8,128]{1,0:T(8,128)S(1)}) custom-call(s32[12,20]{1,0:T(8,128)S(1)} %bitcast.12, s32[2,48]{1,0:T(2,128)S(1)} %bitcast.11, bf16[2560,1536]{1,0:T(8,128)(2,1)S(1)} %copy-done, bf16[6144,256]{1,0:T(8,128)(2,1)S(1)} %copy-done.1), custom_call_target="tpu_custom_call" | custom-call | flops 2013265920 | bytes 18350080 | tf_op jit(solution)/shard_map/own_product/pallas_call | solution.py:64
  16.6 1.4 %collective-permute-done.value_ref = bf16[768,256]{1,0:T(8,128)(2,1)S(1)} collective-permute-done((bf16[768,256]{1,0:T(8,128)(2,1)S(1)}, bf16[768,256]{1,0:T(8,128)(2,1)S(1)}, u32[]{:S(2)}, u32[]{:S(2)}) %collective-permute-start) | collective-permute-done | bytes 393248 | tf_op jit(solution)/shard_map/ppermute | solution.py:231
  18.0 23.6 %collective-permute-start.2 = (bf16[768,256]{1,0:T(8,128)(2,1)S(1)}, bf16[768,256]{1,0:T(8,128)(2,1)S(1)}, u32[]{:S(2)}, u32[]{:S(2)}) collective-permute-start(bf16[768,256]{1,0:T(8,128)(2,1)S(1)} %after.1.once_ref), channel_id=1, source_target_pairs={{129,1},{130,2},{131,3},{132,4},{133,5},{134,6},{135,7},{136,8},{1... | collective-permute-start | bytes 1179656 | tf_op jit(solution)/shard_map/ppermute | solution.py:235
  41.6 0.0 collective-permute-done.1.twice_ref
  41.6 14.8 %collective-permute-done.2.relayed_ref = bf16[768,256]{1,0:T(8,128)(2,1)S(1)} collective-permute-done((bf16[768,256]{1,0:T(8,128)(2,1)S(1)}, bf16[768,256]{1,0:T(8,128)(2,1)S(1)}, u32[]{:S(2)}, u32[]{:S(2)}) %collective-permute-start.2) | collective-permute-done | bytes 393248 | tf_op jit(solution)/shard_map/ppermute | solution.py:235
  56.4 1.5 %away_product.3 = s16[1296,256]{1,0:T(8,128)(2,1)S(1)} custom-call(s32[1]{0:T(128)} %bitcast.2.core_ref, bf16[2560,1536]{1,0:T(8,128)(2,1)S(1)} %get-tuple-element.9.a_ref, bf16[768,256]{1,0:T(8,128)(2,1)S(1)} %after.1.once_ref, bf16[768,256]{1,0:T(8,128)(2,1)S(1)} %collective-permute-done.1.twice_ref, bf16[768,256]{1,0:T(8,128)(2,1)S(1)} %collective-permute-done.2.relayed_ref), custom_call_target="tpu_custom_call" | custom-call | flops 1006632960 | bytes 3932160 | tf_op jit(solution)/shard_map/away_product/pallas_call | solution.py:143
  57.9 8.7 %collective-permute-start.4 = (s16[1296,256]{1,0:T(8,128)(2,1)S(1)}, s16[1296,256]{1,0:T(8,128)(2,1)S(1)}, u32[]{:S(2)}, u32[]{:S(2)}) collective-permute-start(s16[1296,256]{1,0:T(8,128)(2,1)S(1)} %away_product.3), channel_id=1, source_target_pairs={{0,31},{1,0},{2,1},{3,2},{4,3},{5,4},{6,5},{7,6},{8,7},{9,8},{10,9... | collective-permute-start | bytes 1990664 | tf_op jit(solution)/shard_map/ppermute | solution.py:239
  66.6 1.5 %away_product.2 = s16[1296,256]{1,0:T(8,128)(2,1)S(1)} custom-call(s32[1]{0:T(128)} %bitcast.2.core_ref, bf16[2560,1536]{1,0:T(8,128)(2,1)S(1)} %get-tuple-element.9.a_ref, bf16[768,256]{1,0:T(8,128)(2,1)S(1)} %after.1.once_ref, bf16[768,256]{1,0:T(8,128)(2,1)S(1)} %collective-permute-done.1.twice_ref, bf16[768,256]{1,0:T(8,128)(2,1)S(1)} %collective-permute-done.2.relayed_ref), custom_call_target="tpu_custom_call" | custom-call | flops 1006632960 | bytes 3932160 | tf_op jit(solution)/shard_map/away_product/pallas_call | solution.py:143
  68.2 5.3 %collective-permute-start.3 = (s16[1296,256]{1,0:T(8,128)(2,1)S(1)}, s16[1296,256]{1,0:T(8,128)(2,1)S(1)}, u32[]{:S(2)}, u32[]{:S(2)}) collective-permute-start(s16[1296,256]{1,0:T(8,128)(2,1)S(1)} %away_product.2), channel_id=1, source_target_pairs={{0,31},{1,0},{2,1},{3,2},{4,3},{5,4},{6,5},{7,6},{8,7},{9,8},{10,9... | collective-permute-start | bytes 1990664 | tf_op jit(solution)/shard_map/ppermute | solution.py:239
  73.5 22.3 %collective-permute-done.4.coded_ref = s16[1296,256]{1,0:T(8,128)(2,1)S(1)} collective-permute-done((s16[1296,256]{1,0:T(8,128)(2,1)S(1)}, s16[1296,256]{1,0:T(8,128)(2,1)S(1)}, u32[]{:S(2)}, u32[]{:S(2)}) %collective-permute-start.4) | collective-permute-done | bytes 663584 | tf_op jit(solution)/shard_map/ppermute | solution.py:239
  95.8 1.0 join.2.rest_0_
  96.7 11.9 %collective-permute-done.3.coded_ref = s16[1296,256]{1,0:T(8,128)(2,1)S(1)} collective-permute-done((s16[1296,256]{1,0:T(8,128)(2,1)S(1)}, s16[1296,256]{1,0:T(8,128)(2,1)S(1)}, u32[]{:S(2)}, u32[]{:S(2)}) %collective-permute-start.3) | collective-permute-done | bytes 663584 | tf_op jit(solution)/shard_map/ppermute | solution.py:239
  108.6 1.0 join.3
  (6 shorter events, 0.0 us)
Async XLA Ops:
  0.0 9.3 %copy-start.2 = (s32[48,2]{0,1:T(2,128)S(1)}, s32[48,2]{0,1:T(2,128)}, u32[]{:S(2)}) copy-start(s32[48,2]{0,1:T(2,128)} %param.7) | copy-start | bytes 1156
  0.0 9.3 %copy-start.1 = (bf16[6144,256]{1,0:T(8,128)(2,1)S(1)}, bf16[6144,256]{1,0:T(8,128)(2,1)}, u32[]{:S(2)}) copy-start(bf16[6144,256]{1,0:T(8,128)(2,1)} %b_ref.1) | copy-start | bytes 9437188
  0.0 9.3 %copy-start.3 = (s32[20,12]{0,1:T(8,128)S(1)}, s32[20,12]{0,1:T(8,128)}, u32[]{:S(2)}) copy-start(s32[20,12]{0,1:T(8,128)} %param.6) | copy-start | bytes 2884
  3.0 15.0 %collective-permute-start = (bf16[768,256]{1,0:T(8,128)(2,1)S(1)}, bf16[768,256]{1,0:T(8,128)(2,1)S(1)}, u32[]{:S(2)}, u32[]{:S(2)}) collective-permute-start(bf16[768,256]{1,0:T(8,128)(2,1)S(1)} %get-tuple-element.12), channel_id=1, source_target_pairs={{0,225},{1,226},{2,227},{3,228},{4,229},{5,230},{6,231},{7,232},{8... | collective-permute-start | bytes 1179656 | tf_op jit(solution)/shard_map/ppermute | solution.py:231
  8.4 33.2 %collective-permute-start.1 = (bf16[768,256]{1,0:T(8,128)(2,1)S(1)}, bf16[768,256]{1,0:T(8,128)(2,1)S(1)}, u32[]{:S(2)}, u32[]{:S(2)}) collective-permute-start(bf16[768,256]{1,0:T(8,128)(2,1)S(1)} %get-tuple-element.11), channel_id=1, source_target_pairs={{0,225},{1,226},{2,227},{3,228},{4,229},{5,230},{6,231},{7,232},{8... | collective-permute-start | bytes 1179656 | tf_op jit(solution)/shard_map/ppermute | solution.py:232
  9.3 3.2 %copy-start = (bf16[2560,1536]{1,0:T(8,128)(2,1)S(1)}, bf16[2560,1536]{1,0:T(8,128)(2,1)}, u32[]{:S(2)}) copy-start(bf16[2560,1536]{1,0:T(8,128)(2,1)} %a_ref.1) | copy-start | bytes 23592964
  18.0 38.4 %collective-permute-start.2 = (bf16[768,256]{1,0:T(8,128)(2,1)S(1)}, bf16[768,256]{1,0:T(8,128)(2,1)S(1)}, u32[]{:S(2)}, u32[]{:S(2)}) collective-permute-start(bf16[768,256]{1,0:T(8,128)(2,1)S(1)} %after.1.once_ref), channel_id=1, source_target_pairs={{129,1},{130,2},{131,3},{132,4},{133,5},{134,6},{135,7},{136,8},{1... | collective-permute-start | bytes 1179656 | tf_op jit(solution)/shard_map/ppermute | solution.py:235
  57.9 37.8 %collective-permute-start.4 = (s16[1296,256]{1,0:T(8,128)(2,1)S(1)}, s16[1296,256]{1,0:T(8,128)(2,1)S(1)}, u32[]{:S(2)}, u32[]{:S(2)}) collective-permute-start(s16[1296,256]{1,0:T(8,128)(2,1)S(1)} %away_product.3), channel_id=1, source_target_pairs={{0,31},{1,0},{2,1},{3,2},{4,3},{5,4},{6,5},{7,6},{8,7},{9,8},{10,9... | collective-permute-start | bytes 1990664 | tf_op jit(solution)/shard_map/ppermute | solution.py:239
  68.2 40.5 %collective-permute-start.3 = (s16[1296,256]{1,0:T(8,128)(2,1)S(1)}, s16[1296,256]{1,0:T(8,128)(2,1)S(1)}, u32[]{:S(2)}, u32[]{:S(2)}) collective-permute-start(s16[1296,256]{1,0:T(8,128)(2,1)S(1)} %away_product.2), channel_id=1, source_target_pairs={{0,31},{1,0},{2,1},{3,2},{4,3},{5,4},{6,5},{7,6},{8,7},{9,8},{10,9... | collective-permute-start | bytes 1990664 | tf_op jit(solution)/shard_map/ppermute | solution.py:239

commit v4 on v3

--- a/solution.py
+++ b/solution.py
@@ -31,8 +31,8 @@
     place = place_of(row, which)
     piece = lax.dynamic_slice_in_dim(mat_b, place * half, half, 0)
     flags = lax.dynamic_slice_in_dim(mask_b, place * blocks, blocks, 0)
-    kept = piece.reshape(blocks, BLK, columns // BLK, BLK) * flags.astype(mat_b.dtype)[:, None, :, None]
-    return kept.reshape(half, columns)
+    kept = jnp.repeat(jnp.repeat(flags > 0, BLK, 1), BLK, 0)
+    return jnp.where(kept, piece, jnp.zeros_like(piece))
 
 
 def mask_rows(mask_ref, a_ref, held, first_block):

time: 110 us -> 109 us (level)
  local copies, waits for them, and re-layouts: 4 us -> 6.57 us
  starting transfers between devices: 43.9 us -> 42 us
  waiting for transfers between devices: 50.4 us -> 49 us
    unnamed x8, local copies, waits for them, and re-layouts: 3.24 us -> 6.5 us
    ppermute x1, starting transfers between devices: 23.6 us -> 21.7 us  [body(): relayed = lax.ppermute(once, axes, second_leg)]
    ppermute x1, waiting for transfers between devices: 1.37 us -> 0.01 us  [body(): lax.ppermute(pick_b(mat_b, mask_b, place, 0, depth // 2), axes, first_leg)]
    mul x1 -> x0, other arithmetic: 1.31 us -> none  [pick_b(): piece.reshape(blocks, BLK, columns // BLK, BLK)]
    select_n x0 -> x1, other arithmetic: none -> 1.26 us  [pick_b(): return jnp.where(kept, piece, jnp.zeros_like(piece))]
  transfers between devices with their start and end apart: 5 -> 5, of which waited for: 4 -> 3; matrix products, arithmetic and copies ran while one was open for 0% -> 0% of each run, Pallas kernels for 6% -> 6%
where the time goes in v4:
time: 109 us
  waiting for transfers between devices  49 us (45%)
  starting transfers between devices  42 us (39%)
  Pallas kernels  9.04 us (8%)
  local copies, waits for them, and re-layouts  6.57 us (6%)
  other arithmetic  2.09 us (2%)
    ppermute x2, waiting for transfers between devices, body(): arrived.append(lax.ppermute(coded, axes, give_c))  34.2 us
    ppermute x1, starting transfers between devices, body(): relayed = lax.ppermute(once, axes, second_leg)  21.7 us
    ppermute x1, waiting for transfers between devices, body(): relayed = lax.ppermute(once, axes, second_leg)  14.7 us
    ppermute x2, starting transfers between devices, body(): arrived.append(lax.ppermute(coded, axes, give_c))  14 us
    unnamed x8, local copies, waits for them, and re-layouts  6.5 us
    ppermute x1, starting transfers between devices, body(): lax.ppermute(pick_b(mat_b, mask_b, place, 0, depth // 2), axes, first_leg)  5.35 us
    pallas_call x1, Pallas kernels, own_product(): pl.pallas_call(own_kernel, grid_spec=pltpu.PrefetchScalarGridSpec(num_sca...  4.05 us
    pallas_call x2, Pallas kernels, away_product(): pl.pallas_call(away_kernel, grid=(1,), in_specs=[pl.BlockSpec(memory_spac...  3.09 us
  transfers between devices with their start and end apart: 5, of which 3 were waited for; matrix products, arithmetic and copies ran while one was open for 0% of the time, Pallas kernels for 6%

profile of v4, /device:TPU:32, one launch (start us, length us, event | category | flops | bytes accessed | tf_op | source)
XLA Modules:
  0.0 108.7 jit_solution(9499383804975495677)
XLA Ops:
  0.0 0.8 dynamic-slice_compare_fusion
  0.8 0.1 broadcast_bitcast_fusion
  0.9 1.3 %bitcast_select_fusion = (bf16[768,256]{1,0:T(8,128)(2,1)S(1)}, bf16[768,256]{1,0:T(8,128)(2,1)S(1)}) fusion(bf16[6144,256]{1,0:T(8,128)(2,1)} %b_ref.1, s32[]{:T(128)S(6)} %select_n.29, pred[6,256]{1,0:T(8,128)(4,1)S(1)} %get-tuple-element.15, s32[]{:T(128)S(6)} %select_n.26, pred[6,256]{1,0:T(8,128)(4,1)S(1)} %get-tuple-element.16), kind=kLoop, calls=%fused_computation | loop fusion | flops 393216 | bytes 1575944 | tf_op jit(solution)/shard_map/jit(_where)/select_n | solution.py:35
  2.2 5.4 %collective-permute-start = (bf16[768,256]{1,0:T(8,128)(2,1)S(1)}, bf16[768,256]{1,0:T(8,128)(2,1)S(1)}, u32[]{:S(2)}, u32[]{:S(2)}) collective-permute-start(bf16[768,256]{1,0:T(8,128)(2,1)S(1)} %get-tuple-element.12), channel_id=1, source_target_pairs={{0,225},{1,226},{2,227},{3,228},{4,229},{5,230},{6,231},{7,232},{8... | collective-permute-start | bytes 1179656 | tf_op jit(solution)/shard_map/ppermute | solution.py:231
  7.5 0.9 collective-permute-start.1
  8.5 3.2 %copy-done = bf16[2560,1536]{1,0:T(8,128)(2,1)S(1)} copy-done((bf16[2560,1536]{1,0:T(8,128)(2,1)S(1)}, bf16[2560,1536]{1,0:T(8,128)(2,1)}, u32[]{:S(2)}) %copy-start) | copy-done | bytes 7864344
  11.7 0.0 copy-start.1
  11.7 1.9 %copy-done.1 = bf16[6144,256]{1,0:T(8,128)(2,1)S(1)} copy-done((bf16[6144,256]{1,0:T(8,128)(2,1)S(1)}, bf16[6144,256]{1,0:T(8,128)(2,1)}, u32[]{:S(2)}) %copy-start.1) | copy-done | bytes 3145752
  13.6 0.0 copy-start.2
  13.6 0.7 copy-done.2
  14.3 0.7 copy-done.3
  15.0 4.0 %own_product.1 = (f32[2560,256]{1,0:T(8,128)S(1)}, bf16[2560,1536]{1,0:T(8,128)(2,1)S(1)}, f32[8,128]{1,0:T(8,128)S(1)}) custom-call(s32[12,20]{1,0:T(8,128)S(1)} %bitcast.12, s32[2,48]{1,0:T(2,128)S(1)} %bitcast.11, bf16[2560,1536]{1,0:T(8,128)(2,1)S(1)} %copy-done, bf16[6144,256]{1,0:T(8,128)(2,1)S(1)} %copy-done.1), custom_call_target="tpu_custom_call" | custom-call | flops 2013265920 | bytes 18350080 | tf_op jit(solution)/shard_map/own_product/pallas_call | solution.py:64
  19.0 0.0 collective-permute-done.value_ref
  19.0 21.7 %collective-permute-start.2 = (bf16[768,256]{1,0:T(8,128)(2,1)S(1)}, bf16[768,256]{1,0:T(8,128)(2,1)S(1)}, u32[]{:S(2)}, u32[]{:S(2)}) collective-permute-start(bf16[768,256]{1,0:T(8,128)(2,1)S(1)} %after.1.once_ref), channel_id=1, source_target_pairs={{129,1},{130,2},{131,3},{132,4},{133,5},{134,6},{135,7},{136,8},{1... | collective-permute-start | bytes 1179656 | tf_op jit(solution)/shard_map/ppermute | solution.py:235
  40.8 0.0 collective-permute-done.1.twice_ref
  40.8 14.7 %collective-permute-done.2.relayed_ref = bf16[768,256]{1,0:T(8,128)(2,1)S(1)} collective-permute-done((bf16[768,256]{1,0:T(8,128)(2,1)S(1)}, bf16[768,256]{1,0:T(8,128)(2,1)S(1)}, u32[]{:S(2)}, u32[]{:S(2)}) %collective-permute-start.2) | collective-permute-done | bytes 393248 | tf_op jit(solution)/shard_map/ppermute | solution.py:235
  55.5 1.5 %away_product.3 = s16[1296,256]{1,0:T(8,128)(2,1)S(1)} custom-call(s32[1]{0:T(128)} %bitcast.2.core_ref, bf16[2560,1536]{1,0:T(8,128)(2,1)S(1)} %get-tuple-element.9.a_ref, bf16[768,256]{1,0:T(8,128)(2,1)S(1)} %after.1.once_ref, bf16[768,256]{1,0:T(8,128)(2,1)S(1)} %collective-permute-done.1.twice_ref, bf16[768,256]{1,0:T(8,128)(2,1)S(1)} %collective-permute-done.2.relayed_ref), custom_call_target="tpu_custom_call" | custom-call | flops 1006632960 | bytes 3932160 | tf_op jit(solution)/shard_map/away_product/pallas_call | solution.py:143
  57.1 8.7 %collective-permute-start.4 = (s16[1296,256]{1,0:T(8,128)(2,1)S(1)}, s16[1296,256]{1,0:T(8,128)(2,1)S(1)}, u32[]{:S(2)}, u32[]{:S(2)}) collective-permute-start(s16[1296,256]{1,0:T(8,128)(2,1)S(1)} %away_product.3), channel_id=1, source_target_pairs={{0,31},{1,0},{2,1},{3,2},{4,3},{5,4},{6,5},{7,6},{8,7},{9,8},{10,9... | collective-permute-start | bytes 1990664 | tf_op jit(solution)/shard_map/ppermute | solution.py:239
  65.7 1.5 %away_product.2 = s16[1296,256]{1,0:T(8,128)(2,1)S(1)} custom-call(s32[1]{0:T(128)} %bitcast.2.core_ref, bf16[2560,1536]{1,0:T(8,128)(2,1)S(1)} %get-tuple-element.9.a_ref, bf16[768,256]{1,0:T(8,128)(2,1)S(1)} %after.1.once_ref, bf16[768,256]{1,0:T(8,128)(2,1)S(1)} %collective-permute-done.1.twice_ref, bf16[768,256]{1,0:T(8,128)(2,1)S(1)} %collective-permute-done.2.relayed_ref), custom_call_target="tpu_custom_call" | custom-call | flops 1006632960 | bytes 3932160 | tf_op jit(solution)/shard_map/away_product/pallas_call | solution.py:143
  67.3 5.3 %collective-permute-start.3 = (s16[1296,256]{1,0:T(8,128)(2,1)S(1)}, s16[1296,256]{1,0:T(8,128)(2,1)S(1)}, u32[]{:S(2)}, u32[]{:S(2)}) collective-permute-start(s16[1296,256]{1,0:T(8,128)(2,1)S(1)} %away_product.2), channel_id=1, source_target_pairs={{0,31},{1,0},{2,1},{3,2},{4,3},{5,4},{6,5},{7,6},{8,7},{9,8},{10,9... | collective-permute-start | bytes 1990664 | tf_op jit(solution)/shard_map/ppermute | solution.py:239
  72.6 22.3 %collective-permute-done.4.coded_ref = s16[1296,256]{1,0:T(8,128)(2,1)S(1)} collective-permute-done((s16[1296,256]{1,0:T(8,128)(2,1)S(1)}, s16[1296,256]{1,0:T(8,128)(2,1)S(1)}, u32[]{:S(2)}, u32[]{:S(2)}) %collective-permute-start.4) | collective-permute-done | bytes 663584 | tf_op jit(solution)/shard_map/ppermute | solution.py:239
  94.9 1.0 join.2.rest_0_
  95.8 11.9 %collective-permute-done.3.coded_ref = s16[1296,256]{1,0:T(8,128)(2,1)S(1)} collective-permute-done((s16[1296,256]{1,0:T(8,128)(2,1)S(1)}, s16[1296,256]{1,0:T(8,128)(2,1)S(1)}, u32[]{:S(2)}, u32[]{:S(2)}) %collective-permute-start.3) | collective-permute-done | bytes 663584 | tf_op jit(solution)/shard_map/ppermute | solution.py:239
  107.8 1.0 join.3
  (3 shorter events, 0.0 us)
Async XLA Ops:
  2.2 16.9 %collective-permute-start = (bf16[768,256]{1,0:T(8,128)(2,1)S(1)}, bf16[768,256]{1,0:T(8,128)(2,1)S(1)}, u32[]{:S(2)}, u32[]{:S(2)}) collective-permute-start(bf16[768,256]{1,0:T(8,128)(2,1)S(1)} %get-tuple-element.12), channel_id=1, source_target_pairs={{0,225},{1,226},{2,227},{3,228},{4,229},{5,230},{6,231},{7,232},{8... | collective-permute-start | bytes 1179656 | tf_op jit(solution)/shard_map/ppermute | solution.py:231
  7.5 33.2 %collective-permute-start.1 = (bf16[768,256]{1,0:T(8,128)(2,1)S(1)}, bf16[768,256]{1,0:T(8,128)(2,1)S(1)}, u32[]{:S(2)}, u32[]{:S(2)}) collective-permute-start(bf16[768,256]{1,0:T(8,128)(2,1)S(1)} %get-tuple-element.11), channel_id=1, source_target_pairs={{0,225},{1,226},{2,227},{3,228},{4,229},{5,230},{6,231},{7,232},{8... | collective-permute-start | bytes 1179656 | tf_op jit(solution)/shard_map/ppermute | solution.py:232
  8.5 3.2 %copy-start = (bf16[2560,1536]{1,0:T(8,128)(2,1)S(1)}, bf16[2560,1536]{1,0:T(8,128)(2,1)}, u32[]{:S(2)}) copy-start(bf16[2560,1536]{1,0:T(8,128)(2,1)} %a_ref.1) | copy-start | bytes 23592964
  11.7 1.9 %copy-start.1 = (bf16[6144,256]{1,0:T(8,128)(2,1)S(1)}, bf16[6144,256]{1,0:T(8,128)(2,1)}, u32[]{:S(2)}) copy-start(bf16[6144,256]{1,0:T(8,128)(2,1)} %b_ref.1) | copy-start | bytes 9437188
  13.6 0.7 copy-start.2
  14.3 0.7 copy-start.3
  19.0 36.5 %collective-permute-start.2 = (bf16[768,256]{1,0:T(8,128)(2,1)S(1)}, bf16[768,256]{1,0:T(8,128)(2,1)S(1)}, u32[]{:S(2)}, u32[]{:S(2)}) collective-permute-start(bf16[768,256]{1,0:T(8,128)(2,1)S(1)} %after.1.once_ref), channel_id=1, source_target_pairs={{129,1},{130,2},{131,3},{132,4},{133,5},{134,6},{135,7},{136,8},{1... | collective-permute-start | bytes 1179656 | tf_op jit(solution)/shard_map/ppermute | solution.py:235
  57.1 37.8 %collective-permute-start.4 = (s16[1296,256]{1,0:T(8,128)(2,1)S(1)}, s16[1296,256]{1,0:T(8,128)(2,1)S(1)}, u32[]{:S(2)}, u32[]{:S(2)}) collective-permute-start(s16[1296,256]{1,0:T(8,128)(2,1)S(1)} %away_product.3), channel_id=1, source_target_pairs={{0,31},{1,0},{2,1},{3,2},{4,3},{5,4},{6,5},{7,6},{8,7},{9,8},{10,9... | collective-permute-start | bytes 1990664 | tf_op jit(solution)/shard_map/ppermute | solution.py:239
  67.3 40.5 %collective-permute-start.3 = (s16[1296,256]{1,0:T(8,128)(2,1)S(1)}, s16[1296,256]{1,0:T(8,128)(2,1)S(1)}, u32[]{:S(2)}, u32[]{:S(2)}) collective-permute-start(s16[1296,256]{1,0:T(8,128)(2,1)S(1)} %away_product.2), channel_id=1, source_target_pairs={{0,31},{1,0},{2,1},{3,2},{4,3},{5,4},{6,5},{7,6},{8,7},{9,8},{10,9... | collective-permute-start | bytes 1990664 | tf_op jit(solution)/shard_map/ppermute | solution.py:239

commit v5 on v4

--- a/solution.py
+++ b/solution.py
@@ -11,7 +11,7 @@
 STEP_BLOCKS = 5
 PAD = 16
 JOIN_BLOCKS = 5
-PARTS = 2
+PARTS = 4
 MIB = 1024 * 1024
 
 

time: 109 us -> 109 us (level)
  waiting for transfers between devices: 49 us -> 41.1 us
  starting transfers between devices: 42 us -> 48.4 us
  Pallas kernels: 9.04 us -> 11 us
    ppermute x2 -> x4, waiting for transfers between devices: 34.2 us -> 25.1 us  [body(): arrived.append(lax.ppermute(coded, axes, give_c))]
    ppermute x2 -> x4, starting transfers between devices: 14 us -> 20.4 us  [body(): arrived.append(lax.ppermute(coded, axes, give_c))]
    pallas_call x2 -> x4, Pallas kernels: 1.91 us -> 3.32 us  [join(): pl.pallas_call(functools.partial(join_kernel, start=part * steps * JOIN_B...]
    ppermute x1, waiting for transfers between devices: 14.7 us -> 16 us  [body(): relayed = lax.ppermute(once, axes, second_leg)]
    pallas_call x2 -> x4, Pallas kernels: 3.09 us -> 3.59 us  [away_product(): pl.pallas_call(away_kernel, grid=(1,), in_specs=[pl.BlockSpec(memory_spac...]
  transfers between devices with their start and end apart: 5 -> 7, of which waited for: 3 -> 3; matrix products, arithmetic and copies ran while one was open for 0% -> 0% of each run, Pallas kernels for 6% -> 8%
where the time goes in v5:
time: 109 us
  starting transfers between devices  48.4 us (44%)
  waiting for transfers between devices  41.1 us (38%)
  Pallas kernels  11 us (10%)
  local copies, waits for them, and re-layouts  6.57 us (6%)
  other arithmetic  2.09 us (2%)
    ppermute x4, waiting for transfers between devices, body(): arrived.append(lax.ppermute(coded, axes, give_c))  25.1 us
    ppermute x1, starting transfers between devices, body(): relayed = lax.ppermute(once, axes, second_leg)  21.7 us
    ppermute x4, starting transfers between devices, body(): arrived.append(lax.ppermute(coded, axes, give_c))  20.4 us
    ppermute x1, waiting for transfers between devices, body(): relayed = lax.ppermute(once, axes, second_leg)  16 us
    unnamed x8, local copies, waits for them, and re-layouts  6.5 us
    ppermute x1, starting transfers between devices, body(): lax.ppermute(pick_b(mat_b, mask_b, place, 0, depth // 2), axes, first_leg)  5.35 us
    pallas_call x1, Pallas kernels, own_product(): pl.pallas_call(own_kernel, grid_spec=pltpu.PrefetchScalarGridSpec(num_sca...  4.05 us
    pallas_call x4, Pallas kernels, away_product(): pl.pallas_call(away_kernel, grid=(1,), in_specs=[pl.BlockSpec(memory_spac...  3.59 us
  transfers between devices with their start and end apart: 7, of which 3 were waited for; matrix products, arithmetic and copies ran while one was open for 0% of the time, Pallas kernels for 8%

profile of v5, /device:TPU:32, one launch (start us, length us, event | category | flops | bytes accessed | tf_op | source)
XLA Modules:
  0.0 109.2 jit_solution(15792405671845597619)
XLA Ops:
  0.0 0.8 dynamic-slice_compare_fusion
  0.9 1.3 %bitcast_select_fusion = (bf16[768,256]{1,0:T(8,128)(2,1)S(1)}, bf16[768,256]{1,0:T(8,128)(2,1)S(1)}) fusion(bf16[6144,256]{1,0:T(8,128)(2,1)} %b_ref.1, s32[]{:T(128)S(6)} %select_n.29, pred[6,256]{1,0:T(8,128)(4,1)S(1)} %get-tuple-element.15, s32[]{:T(128)S(6)} %select_n.26, pred[6,256]{1,0:T(8,128)(4,1)S(1)} %get-tuple-element.16), kind=kLoop, calls=%fused_computation | loop fusion | flops 393216 | bytes 1575944 | tf_op jit(solution)/shard_map/jit(_where)/select_n | solution.py:35
  2.2 5.4 %collective-permute-start = (bf16[768,256]{1,0:T(8,128)(2,1)S(1)}, bf16[768,256]{1,0:T(8,128)(2,1)S(1)}, u32[]{:S(2)}, u32[]{:S(2)}) collective-permute-start(bf16[768,256]{1,0:T(8,128)(2,1)S(1)} %get-tuple-element.12), channel_id=1, source_target_pairs={{0,225},{1,226},{2,227},{3,228},{4,229},{5,230},{6,231},{7,232},{8... | collective-permute-start | bytes 1179656 | tf_op jit(solution)/shard_map/ppermute | solution.py:231
  7.5 0.9 collective-permute-start.1
  8.5 3.2 %copy-done = bf16[2560,1536]{1,0:T(8,128)(2,1)S(1)} copy-done((bf16[2560,1536]{1,0:T(8,128)(2,1)S(1)}, bf16[2560,1536]{1,0:T(8,128)(2,1)}, u32[]{:S(2)}) %copy-start) | copy-done | bytes 7864344
  11.7 1.9 %copy-done.1 = bf16[6144,256]{1,0:T(8,128)(2,1)S(1)} copy-done((bf16[6144,256]{1,0:T(8,128)(2,1)S(1)}, bf16[6144,256]{1,0:T(8,128)(2,1)}, u32[]{:S(2)}) %copy-start.1) | copy-done | bytes 3145752
  14.3 0.7 copy-done.3
  15.0 4.0 %own_product.1 = (f32[2560,256]{1,0:T(8,128)S(1)}, bf16[2560,1536]{1,0:T(8,128)(2,1)S(1)}, f32[8,128]{1,0:T(8,128)S(1)}) custom-call(s32[12,20]{1,0:T(8,128)S(1)} %bitcast.12, s32[2,48]{1,0:T(2,128)S(1)} %bitcast.11, bf16[2560,1536]{1,0:T(8,128)(2,1)S(1)} %copy-done, bf16[6144,256]{1,0:T(8,128)(2,1)S(1)} %copy-done.1), custom_call_target="tpu_custom_call" | custom-call | flops 2013265920 | bytes 18350080 | tf_op jit(solution)/shard_map/own_product/pallas_call | solution.py:64
  19.0 21.7 %collective-permute-start.2 = (bf16[768,256]{1,0:T(8,128)(2,1)S(1)}, bf16[768,256]{1,0:T(8,128)(2,1)S(1)}, u32[]{:S(2)}, u32[]{:S(2)}) collective-permute-start(bf16[768,256]{1,0:T(8,128)(2,1)S(1)} %after.1.once_ref), channel_id=1, source_target_pairs={{129,1},{130,2},{131,3},{132,4},{133,5},{134,6},{135,7},{136,8},{1... | collective-permute-start | bytes 1179656 | tf_op jit(solution)/shard_map/ppermute | solution.py:235
  40.8 16.0 %collective-permute-done.2.relayed_ref = bf16[768,256]{1,0:T(8,128)(2,1)S(1)} collective-permute-done((bf16[768,256]{1,0:T(8,128)(2,1)S(1)}, bf16[768,256]{1,0:T(8,128)(2,1)S(1)}, u32[]{:S(2)}, u32[]{:S(2)}) %collective-permute-start.2) | collective-permute-done | bytes 393248 | tf_op jit(solution)/shard_map/ppermute | solution.py:235
  56.8 0.9 away_product.5
  57.7 7.7 %collective-permute-start.4 = (s16[656,256]{1,0:T(8,128)(2,1)S(1)}, s16[656,256]{1,0:T(8,128)(2,1)S(1)}, u32[]{:S(2)}, u32[]{:S(2)}) collective-permute-start(s16[656,256]{1,0:T(8,128)(2,1)S(1)} %away_product.5), channel_id=1, source_target_pairs={{0,31},{1,0},{2,1},{3,2},{4,3},{5,4},{6,5},{7,6},{8,7},{9,8},{10,9... | collective-permute-start | bytes 1007624 | tf_op jit(solution)/shard_map/ppermute | solution.py:239
  65.4 0.9 away_product.6
  66.3 5.6 %collective-permute-start.5 = (s16[656,256]{1,0:T(8,128)(2,1)S(1)}, s16[656,256]{1,0:T(8,128)(2,1)S(1)}, u32[]{:S(2)}, u32[]{:S(2)}) collective-permute-start(s16[656,256]{1,0:T(8,128)(2,1)S(1)} %away_product.6), channel_id=1, source_target_pairs={{0,31},{1,0},{2,1},{3,2},{4,3},{5,4},{6,5},{7,6},{8,7},{9,8},{10,9... | collective-permute-start | bytes 1007624 | tf_op jit(solution)/shard_map/ppermute | solution.py:239
  71.9 0.9 away_product.7
  72.8 2.0 %collective-permute-start.6 = (s16[656,256]{1,0:T(8,128)(2,1)S(1)}, s16[656,256]{1,0:T(8,128)(2,1)S(1)}, u32[]{:S(2)}, u32[]{:S(2)}) collective-permute-start(s16[656,256]{1,0:T(8,128)(2,1)S(1)} %away_product.7), channel_id=1, source_target_pairs={{0,31},{1,0},{2,1},{3,2},{4,3},{5,4},{6,5},{7,6},{8,7},{9,8},{10,9... | collective-permute-start | bytes 1007624 | tf_op jit(solution)/shard_map/ppermute | solution.py:239
  74.8 0.9 away_product.4
  75.7 5.1 %collective-permute-start.3 = (s16[656,256]{1,0:T(8,128)(2,1)S(1)}, s16[656,256]{1,0:T(8,128)(2,1)S(1)}, u32[]{:S(2)}, u32[]{:S(2)}) collective-permute-start(s16[656,256]{1,0:T(8,128)(2,1)S(1)} %away_product.4), channel_id=1, source_target_pairs={{0,31},{1,0},{2,1},{3,2},{4,3},{5,4},{6,5},{7,6},{8,7},{9,8},{10,9... | collective-permute-start | bytes 1007624 | tf_op jit(solution)/shard_map/ppermute | solution.py:239
  80.8 22.6 %collective-permute-done.6.coded_ref = s16[656,256]{1,0:T(8,128)(2,1)S(1)} collective-permute-done((s16[656,256]{1,0:T(8,128)(2,1)S(1)}, s16[656,256]{1,0:T(8,128)(2,1)S(1)}, u32[]{:S(2)}, u32[]{:S(2)}) %collective-permute-start.6) | collective-permute-done | bytes 335904 | tf_op jit(solution)/shard_map/ppermute | solution.py:239
  103.3 0.8 join.4.rest_0_
  104.2 0.8 join.5.rest_0_
  105.0 0.8 join.6.rest_0_
  105.8 2.5 %collective-permute-done.3.coded_ref = s16[656,256]{1,0:T(8,128)(2,1)S(1)} collective-permute-done((s16[656,256]{1,0:T(8,128)(2,1)S(1)}, s16[656,256]{1,0:T(8,128)(2,1)S(1)}, u32[]{:S(2)}, u32[]{:S(2)}) %collective-permute-start.3) | collective-permute-done | bytes 335904 | tf_op jit(solution)/shard_map/ppermute | solution.py:239
  108.3 0.8 join.7
  (11 shorter events, 0.8 us)
Async XLA Ops:
  2.2 16.9 %collective-permute-start = (bf16[768,256]{1,0:T(8,128)(2,1)S(1)}, bf16[768,256]{1,0:T(8,128)(2,1)S(1)}, u32[]{:S(2)}, u32[]{:S(2)}) collective-permute-start(bf16[768,256]{1,0:T(8,128)(2,1)S(1)} %get-tuple-element.12), channel_id=1, source_target_pairs={{0,225},{1,226},{2,227},{3,228},{4,229},{5,230},{6,231},{7,232},{8... | collective-permute-start | bytes 1179656 | tf_op jit(solution)/shard_map/ppermute | solution.py:231
  7.5 33.3 %collective-permute-start.1 = (bf16[768,256]{1,0:T(8,128)(2,1)S(1)}, bf16[768,256]{1,0:T(8,128)(2,1)S(1)}, u32[]{:S(2)}, u32[]{:S(2)}) collective-permute-start(bf16[768,256]{1,0:T(8,128)(2,1)S(1)} %get-tuple-element.11), channel_id=1, source_target_pairs={{0,225},{1,226},{2,227},{3,228},{4,229},{5,230},{6,231},{7,232},{8... | collective-permute-start | bytes 1179656 | tf_op jit(solution)/shard_map/ppermute | solution.py:232
  8.5 3.2 %copy-start = (bf16[2560,1536]{1,0:T(8,128)(2,1)S(1)}, bf16[2560,1536]{1,0:T(8,128)(2,1)}, u32[]{:S(2)}) copy-start(bf16[2560,1536]{1,0:T(8,128)(2,1)} %a_ref.1) | copy-start | bytes 23592964
  11.7 1.9 %copy-start.1 = (bf16[6144,256]{1,0:T(8,128)(2,1)S(1)}, bf16[6144,256]{1,0:T(8,128)(2,1)}, u32[]{:S(2)}) copy-start(bf16[6144,256]{1,0:T(8,128)(2,1)} %b_ref.1) | copy-start | bytes 9437188
  13.6 0.7 copy-start.2
  14.3 0.7 copy-start.3
  19.0 37.7 %collective-permute-start.2 = (bf16[768,256]{1,0:T(8,128)(2,1)S(1)}, bf16[768,256]{1,0:T(8,128)(2,1)S(1)}, u32[]{:S(2)}, u32[]{:S(2)}) collective-permute-start(bf16[768,256]{1,0:T(8,128)(2,1)S(1)} %after.1.once_ref), channel_id=1, source_target_pairs={{129,1},{130,2},{131,3},{132,4},{133,5},{134,6},{135,7},{136,8},{1... | collective-permute-start | bytes 1179656 | tf_op jit(solution)/shard_map/ppermute | solution.py:235
  57.7 47.3 %collective-permute-start.4 = (s16[656,256]{1,0:T(8,128)(2,1)S(1)}, s16[656,256]{1,0:T(8,128)(2,1)S(1)}, u32[]{:S(2)}, u32[]{:S(2)}) collective-permute-start(s16[656,256]{1,0:T(8,128)(2,1)S(1)} %away_product.5), channel_id=1, source_target_pairs={{0,31},{1,0},{2,1},{3,2},{4,3},{5,4},{6,5},{7,6},{8,7},{9,8},{10,9... | collective-permute-start | bytes 1007624 | tf_op jit(solution)/shard_map/ppermute | solution.py:239
  66.3 37.9 %collective-permute-start.5 = (s16[656,256]{1,0:T(8,128)(2,1)S(1)}, s16[656,256]{1,0:T(8,128)(2,1)S(1)}, u32[]{:S(2)}, u32[]{:S(2)}) collective-permute-start(s16[656,256]{1,0:T(8,128)(2,1)S(1)} %away_product.6), channel_id=1, source_target_pairs={{0,31},{1,0},{2,1},{3,2},{4,3},{5,4},{6,5},{7,6},{8,7},{9,8},{10,9... | collective-permute-start | bytes 1007624 | tf_op jit(solution)/shard_map/ppermute | solution.py:239
  72.8 30.6 %collective-permute-start.6 = (s16[656,256]{1,0:T(8,128)(2,1)S(1)}, s16[656,256]{1,0:T(8,128)(2,1)S(1)}, u32[]{:S(2)}, u32[]{:S(2)}) collective-permute-start(s16[656,256]{1,0:T(8,128)(2,1)S(1)} %away_product.7), channel_id=1, source_target_pairs={{0,31},{1,0},{2,1},{3,2},{4,3},{5,4},{6,5},{7,6},{8,7},{9,8},{10,9... | collective-permute-start | bytes 1007624 | tf_op jit(solution)/shard_map/ppermute | solution.py:239
  75.7 32.7 %collective-permute-start.3 = (s16[656,256]{1,0:T(8,128)(2,1)S(1)}, s16[656,256]{1,0:T(8,128)(2,1)S(1)}, u32[]{:S(2)}, u32[]{:S(2)}) collective-permute-start(s16[656,256]{1,0:T(8,128)(2,1)S(1)} %away_product.4), channel_id=1, source_target_pairs={{0,31},{1,0},{2,1},{3,2},{4,3},{5,4},{6,5},{7,6},{8,7},{9,8},{10,9... | collective-permute-start | bytes 1007624 | tf_op jit(solution)/shard_map/ppermute | solution.py:239
